TPU v7x, 32 devices: a whole 2x2x4 slice. The times are simulated.
32 devices in a mesh: dp: 8 (over z, x), seq: 4 (over y, core).
Axes of the slice: x: 2, y: 2, z: 4, core: 2. Of those that a mesh axis runs over, the one named last changes fastest.
Arguments:
- short_in: bfloat16 [2, 32, 256, 768], P(None, 'dp', 'seq'), may hold values from -6 to 6
- long_in: bfloat16 [2, 16, 512, 768], P(None, 'dp', 'seq'), may hold values from -6 to 6
- short_cot: bfloat16 [2, 32, 256, 768], P(None, 'dp', 'seq'), may hold values from -6 to 6
- long_cot: bfloat16 [2, 16, 512, 768], P(None, 'dp', 'seq'), may hold values from -6 to 6
- short_len: int32 [2, 8, 4], P(None, 'dp'), may hold values from 0 to 256, as said below
- long_len: int32 [2, 8, 2], P(None, 'dp'), may hold values from 0 to 512, as said below
- wide_master: float32 [768, 6144], P('dp')
- down_master: float32 [3072, 768], P('dp'), may hold values from -0.109375 to 0.109375
- vector_master: float32 [768, 12], P('dp')
- wide_moment: float32 [768, 6144], P('dp'), may hold values from -256 to 256
- down_moment: float32 [3072, 768], P('dp'), may hold values from -256 to 256
- vector_moment: float32 [768, 12], P('dp'), may hold values from -256 to 256
- wide_average: float32 [768, 6144], P('dp'), may hold values from -0.21875 to 0.21875
- down_average: float32 [3072, 768], P('dp'), may hold values from -0.109375 to 0.109375
- vector_average: float32 [768, 12], P('dp'), may hold values from -6 to 6
Outputs:
- short_out: bfloat16 [2, 32, 256, 768], P(None, 'dp', 'seq')
- long_out: bfloat16 [2, 16, 512, 768], P(None, 'dp', 'seq')
- short_back: bfloat16 [2, 32, 256, 768], P(None, 'dp', 'seq')
- long_back: bfloat16 [2, 16, 512, 768], P(None, 'dp', 'seq')
- wide_grad: float32 [768, 6144], P('dp')
- down_grad: float32 [3072, 768], P('dp')
- vector_grad: float32 [768, 12], P('dp')
- wide_velocity: float32 [768, 6144], P('dp')
- down_velocity: float32 [3072, 768], P('dp')
- vector_velocity: float32 [768, 12], P('dp')
- wide_averaged: float32 [768, 6144], P('dp')
- down_averaged: float32 [3072, 768], P('dp')
- vector_averaged: float32 [768, 12], P('dp')
- wide_updated: float32 [768, 6144], P('dp')
- down_updated: float32 [3072, 768], P('dp')
- vector_updated: float32 [768, 12], P('dp')
- wide_copy: bfloat16 [768, 6144], P('dp')
- down_copy: bfloat16 [3072, 768], P('dp')
- vector_copy: bfloat16 [768, 12], P('dp')
Inputs may be any that keep to these rules, and one draw needn't show every extreme that they name: `short_len`: 0 marks an empty slot; in each micro-batch every index of dp has at least half of its slots live and one sequence of exactly 256 tokens. `long_len`: 0 marks an empty slot; in each micro-batch every index of dp has at least half of its slots live and one sequence of exactly 512 tokens.
All inputs are finite; a program needn't handle non-finite values.
Results may differ from a plain program's by a relative error of at most 0.015.
Values may be sent and summed in bfloat16 or wider, within the bound.
A program may use at most 256 MiB of HBM per device.

v0:
```python
import jax
import jax.numpy as jnp
from jax import lax
from jax.experimental import pallas as pl
from jax.experimental.pallas import tpu as pltpu
from jax.sharding import PartitionSpec as P

D = 768
HEAD_DIM = 64
FF = 3072
PAIR = 128
LONG_L = 512
SHORT_L = 256
VMEM_BYTES = 62 * 1024 * 1024

norm_eps = 1e-12
mask_fill = -10000.0
learning_rate = 0.0002
momentum_rate = 0.9
decay_weight = 0.0001
average_rate = 0.9
score_scale = HEAD_DIM ** (-0.5)
FILL_PARTS = (-9984.0, -16.0)
f32 = jnp.float32
bf16 = jnp.bfloat16


def params():
    return pltpu.CompilerParams(vmem_limit_bytes=VMEM_BYTES)


def dot_nn(a, b):
    return lax.dot_general(a, b, (((1,), (0,)), ((), ())), preferred_element_type=f32)


def dot_nt(a, b):
    return lax.dot_general(a, b, (((1,), (1,)), ((), ())), preferred_element_type=f32)


SEQS = ((0, 128, LONG_L, 0), (128, 64, SHORT_L, 1), (192, 64, SHORT_L, 2))


def attend(q, k, v, limit, keep_probs):
    length = q.shape[0]
    v_t = jnp.transpose(v)
    head_lane = lax.broadcasted_iota(jnp.int32, (length, PAIR), 1) // HEAD_DIM
    live = lax.broadcasted_iota(jnp.int32, (length, length), 0) < limit
    parts = []
    for h in range(2):
        k_h = jnp.where(head_lane == h, k, jnp.zeros_like(k))
        scores = jnp.where(live, dot_nt(k_h, q) * score_scale, mask_fill)
        top = jnp.max(scores, axis=0, keepdims=True)
        exponent = jnp.exp(scores - top)
        total = jnp.sum(exponent, axis=0, keepdims=True)
        probs = (exponent * (1.0 / total)).astype(bf16)
        keep_probs(h, probs)
        parts.append(dot_nn(v_t[h * HEAD_DIM : (h + 1) * HEAD_DIM], probs))
    return jnp.transpose(jnp.concatenate(parts, axis=0)).astype(bf16)


def attn_forward_kernel(lens_ref, q_ref, k_ref, v_ref, o_ref, long_ref, short_ref):
    for first, rows, length, index in SEQS:
        q, k, v = [r[:, first : first + rows, :].reshape(length, PAIR) for r in (q_ref, k_ref, v_ref)]

        def keep_probs(h, probs, index=index):
            if index == 0:
                long_ref[h] = probs
            else:
                short_ref[h, index - 1] = probs

        o = attend(q, k, v, lens_ref[index], keep_probs)
        o_ref[:, first : first + rows, :] = o.reshape(4, rows, PAIR)


def attn_forward(lens, qkv):
    pairs = D // PAIR
    col = lambda base: pl.BlockSpec((4, 256, PAIR), lambda i, base=base: (0, 0, base + i))
    return pl.pallas_call(
        attn_forward_kernel,
        grid=(pairs,),
        in_specs=[
            pl.BlockSpec(memory_space=pltpu.SMEM),
            col(0),
            col(pairs),
            col(2 * pairs),
        ],
        out_specs=[
            pl.BlockSpec((4, 256, PAIR), lambda i: (0, 0, i)),
            pl.BlockSpec((2, LONG_L, LONG_L), lambda i: (i, 0, 0)),
            pl.BlockSpec((2, 2, SHORT_L, SHORT_L), lambda i: (i, 0, 0, 0)),
        ],
        out_shape=[
            jax.ShapeDtypeStruct((4, 256, D), bf16),
            jax.ShapeDtypeStruct((2 * pairs, LONG_L, LONG_L), bf16),
            jax.ShapeDtypeStruct((2 * pairs, 2, SHORT_L, SHORT_L), bf16),
        ],
        compiler_params=params(),
        name="attn_forward",
    )(lens, qkv, qkv, qkv)


def attend_back(q, k, v, do, o, limit, kept_probs):
    length = q.shape[0]
    k_t = jnp.transpose(k)
    inner = jnp.transpose(do.astype(f32) * o.astype(f32))
    head_lane = lax.broadcasted_iota(jnp.int32, (length, PAIR), 1) // HEAD_DIM
    live = lax.broadcasted_iota(jnp.int32, (length, length), 0) < limit
    dq_parts = []
    dk = jnp.zeros((length, PAIR), f32)
    dv = jnp.zeros((length, PAIR), f32)
    for h in range(2):
        keep = head_lane == h
        v_h, do_h, q_h = [jnp.where(keep, m, jnp.zeros_like(m)) for m in (v, do, q)]
        probs = kept_probs(h)
        delta = jnp.sum(inner[h * HEAD_DIM : (h + 1) * HEAD_DIM], axis=0, keepdims=True)
        d_probs = dot_nt(v_h, do)
        d_scores = jnp.where(live, probs.astype(f32) * (d_probs - delta), 0.0).astype(bf16)
        dv = dv + dot_nn(probs, do_h)
        dk = dk + dot_nn(d_scores, q_h)
        dq_parts.append(dot_nn(k_t[h * HEAD_DIM : (h + 1) * HEAD_DIM], d_scores))
    dq = jnp.transpose(jnp.concatenate(dq_parts, axis=0)) * score_scale
    return dq.astype(bf16), (dk * score_scale).astype(bf16), dv.astype(bf16)


def attn_backward_kernel(
    lens_ref, q_ref, k_ref, v_ref, do_ref, o_ref, long_ref, short_ref, dq_ref, dk_ref, dv_ref, sum_ref
):
    sum_q = jnp.zeros((1, PAIR), f32)
    sum_v = jnp.zeros((1, PAIR), f32)
    for first, rows, length, index in SEQS:
        args = [r[:, first : first + rows, :].reshape(length, PAIR) for r in (q_ref, k_ref, v_ref, do_ref, o_ref)]
        kept = lambda h, index=index: long_ref[h] if index == 0 else short_ref[h, index - 1]
        dq, dk, dv = attend_back(*args, lens_ref[index], kept)
        sum_q = sum_q + jnp.sum(dq.astype(f32), axis=0, keepdims=True)
        sum_v = sum_v + jnp.sum(dv.astype(f32), axis=0, keepdims=True)
        for ref, v in ((dq_ref, dq), (dk_ref, dk), (dv_ref, dv)):
            ref[:, first : first + rows, :] = v.reshape(4, rows, PAIR)
    sum_ref[0:1, :] = sum_q
    sum_ref[1:2, :] = sum_v
    sum_ref[2:8, :] = jnp.zeros((6, PAIR), f32)


def attn_backward(lens, qkv, d_attended, attended, long_probs, short_probs):
    pairs = D // PAIR
    col = lambda base: pl.BlockSpec((4, 256, PAIR), lambda i, base=base: (0, 0, base + i))
    return pl.pallas_call(
        attn_backward_kernel,
        grid=(pairs,),
        in_specs=[
            pl.BlockSpec(memory_space=pltpu.SMEM),
            col(0),
            col(pairs),
            col(2 * pairs),
            col(0),
            col(0),
            pl.BlockSpec((2, LONG_L, LONG_L), lambda i: (i, 0, 0)),
            pl.BlockSpec((2, 2, SHORT_L, SHORT_L), lambda i: (i, 0, 0, 0)),
        ],
        out_specs=[col(0), col(0), col(0), pl.BlockSpec((8, PAIR), lambda i: (0, i))],
        out_shape=[jax.ShapeDtypeStruct((4, 256, D), bf16)] * 3 + [jax.ShapeDtypeStruct((8, D), f32)],
        compiler_params=params(),
        name="attn_backward",
    )(lens, qkv, qkv, qkv, d_attended, attended, long_probs, short_probs)


def gelu_pair(u):
    t = 1.0 / (1.0 + (0.3275911 * 0.5**0.5) * jnp.abs(u))
    e = jnp.exp2((u * u) * (-0.5 * 1.4426950408889634))
    poly = 0.5 * -0.284496736 + t * (0.5 * 1.421413741 + t * (0.5 * -1.453152027 + t * (0.5 * 1.061405429)))
    tail = (t * (0.5 * 0.254829592 + t * poly)) * e
    cdf = jnp.where(u < 0.0, tail, 1.0 - tail)
    return u * cdf, cdf + (u * (0.5 / jnp.pi) ** 0.5) * e


def row_mean(v):
    return jnp.mean(v, axis=-1, keepdims=True)


def middle_kernel(
    lens_ref,
    o_ref,
    x_ref,
    cot_ref,
    wo_ref,
    w1_ref,
    w2_ref,
    vec_ref,
    out_ref,
    y1b_ref,
    g_ref,
    dfb_ref,
    dub_ref,
    dab_ref,
    dob_ref,
    dh_ref,
    sum_ref,
    slope_ref,
):
    r = pl.program_id(0)
    rows = o_ref.shape[0]

    @pl.when(r == 0)
    def _():
        sum_ref[...] = jnp.zeros_like(sum_ref)

    def add(index, v):
        sum_ref[index : index + 1, :] += jnp.sum(v, axis=0, keepdims=True)

    vec = lambda i: vec_ref[i : i + 1, :]
    h = x_ref[...].astype(f32) + (dot_nn(o_ref[...], wo_ref[...]) + vec(2))
    centred = h - row_mean(h)
    inv1 = lax.rsqrt(row_mean(centred * centred) + norm_eps)
    norm1 = centred * inv1
    y1 = norm1 * vec(3) + vec(4)
    y1b = y1.astype(bf16)
    y1b_ref[...] = y1b
    z = y1 + vec(5)
    for c in range(FF // D):
        cols = slice(c * D, (c + 1) * D)
        act, slope = gelu_pair(dot_nn(y1b, w1_ref[:, cols]) + vec(8 + c))
        act = act.astype(bf16)
        g_ref[:, cols] = act
        slope_ref[:, cols] = slope
        z = z + dot_nn(act, w2_ref[cols, :])
    centred2 = z - row_mean(z)
    inv2 = lax.rsqrt(row_mean(centred2 * centred2) + norm_eps)
    norm2 = centred2 * inv2
    out_ref[...] = (norm2 * vec(6) + vec(7)).astype(bf16)

    j = lax.broadcasted_iota(jnp.int32, (rows, 1), 0)
    long_end = lens_ref[0] - r * 128
    short_end = [lens_ref[i] - r * 64 + first for i, first in ((1, 128), (2, 192))]
    live = j < jnp.where(j < 128, long_end, jnp.where(j < 192, short_end[0], short_end[1]))
    dr = jnp.where(live, cot_ref[...].astype(f32), 0.0)
    e2 = dr * vec(6)
    dz = inv2 * (e2 - row_mean(e2) - norm2 * row_mean(e2 * norm2))
    dfb = dz.astype(bf16)
    dfb_ref[...] = dfb
    add(6, dr * norm2)
    add(7, dr)
    add(5, dfb.astype(f32))
    dy1 = dz
    for c in range(FF // D):
        cols = slice(c * D, (c + 1) * D)
        dub = (dot_nt(dfb, w2_ref[cols, :]) * slope_ref[:, cols]).astype(bf16)
        dub_ref[:, cols] = dub
        add(8 + c, dub.astype(f32))
        dy1 = dy1 + dot_nt(dub, w1_ref[:, cols])
    add(3, dy1 * norm1)
    add(4, dy1)
    e1 = dy1 * vec(3)
    dh = inv1 * (e1 - row_mean(e1) - norm1 * row_mean(e1 * norm1))
    dab = dh.astype(bf16)
    dh_ref[...] = dh
    dab_ref[...] = dab
    add(2, dab.astype(f32))
    dob_ref[...] = dot_nt(dab, wo_ref[...]).astype(bf16)


def middle(lens, attended, tokens, cotangent, w_o, w_1, w_2, vec):
    n = tokens.shape[0]
    rows = 256
    row = lambda width: pl.BlockSpec((rows, width), lambda i: (i, 0))
    whole = lambda a: pl.BlockSpec(a.shape, lambda i: (0, 0), pipeline_mode=pl.Buffered(1))
    shape = jax.ShapeDtypeStruct
    return pl.pallas_call(
        middle_kernel,
        grid=(n // rows,),
        in_specs=[
            pl.BlockSpec(memory_space=pltpu.SMEM),
            row(D),
            row(D),
            row(D),
            whole(w_o),
            whole(w_1),
            whole(w_2),
            whole(vec),
        ],
        out_specs=[
            row(D),
            row(D),
            row(FF),
            row(D),
            row(FF),
            row(D),
            row(D),
            row(D),
            pl.BlockSpec((16, D), lambda i: (0, 0)),
        ],
        out_shape=[
            shape((n, D), bf16),
            shape((n, D), bf16),
            shape((n, FF), bf16),
            shape((n, D), bf16),
            shape((n, FF), bf16),
            shape((n, D), bf16),
            shape((n, D), bf16),
            shape((n, D), f32),
            shape((16, D), f32),
        ],
        scratch_shapes=[pltpu.VMEM((rows, FF), f32)],
        compiler_params=params(),
        name="middle",
    )(lens, attended, tokens, cotangent, w_o, w_1, w_2, vec)


MESH = pl.DeviceIdType.MESH
Z_CHIPS = 4


def place():
    dp = lax.axis_index("dp")
    s = lax.axis_index("seq")
    return dp, s, dp // 2, dp % 2, s // 2, s % 2


def remote(src, dst, send, recv, device):
    return pltpu.make_async_remote_copy(
        src_ref=src, dst_ref=dst, send_sem=send, recv_sem=recv, device_id=device, device_id_type=MESH
    )


def greet():
    dp, s = lax.axis_index("dp"), lax.axis_index("seq")
    barrier = pltpu.get_barrier_semaphore()
    for k in range(1, 8):
        pl.semaphore_signal(barrier, inc=1, device_id=((dp + k) % 8, s), device_id_type=MESH)
    for k in range(1, 4):
        pl.semaphore_signal(barrier, inc=1, device_id=(dp, (s + k) % 4), device_id_type=MESH)
    pl.semaphore_wait(barrier, 10)


def head_operands(q, k, limit, h):
    lane = lax.broadcasted_iota(jnp.int32, q.shape, 1)
    live = lax.broadcasted_iota(jnp.int32, q.shape, 0) < limit
    keep = lane // HEAD_DIM == h
    spare = (1 - h) * HEAD_DIM
    zero = jnp.zeros_like(q)
    fill = jnp.where(lane == spare, jnp.full_like(q, FILL_PARTS[0]), zero)
    fill = jnp.where(lane == spare + 1, jnp.full_like(q, FILL_PARTS[1]), fill)
    k_h = jnp.where(live, jnp.where(keep, k, zero), fill)
    ones = jnp.where((lane == spare) | (lane == spare + 1), jnp.ones_like(q), zero)
    return jnp.where(keep, q * bf16(score_scale), ones), k_h


def attend_sums(q, k, v, limit, keep_exps):
    length = q.shape[0]
    v_t = jnp.transpose(v)
    parts = []
    inverses = []
    for h in range(2):
        q_h, k_h = head_operands(q, k, limit, h)
        scores = dot_nt(k_h, q_h)
        exponent = jnp.exp(scores - jnp.max(scores, axis=0, keepdims=True))
        inverse = 1.0 / jnp.sum(exponent, axis=0, keepdims=True)
        exps = exponent.astype(bf16)
        keep_exps(h, exps)
        parts.append(dot_nn(v_t[h * HEAD_DIM : (h + 1) * HEAD_DIM], exps) * inverse)
        inverses.append(jnp.broadcast_to(inverse, (HEAD_DIM, length)))
    o = jnp.transpose(jnp.concatenate(parts, axis=0)).astype(bf16)
    return o, jnp.transpose(jnp.concatenate(inverses, axis=0))


def attend_sums_back(q, k, v, do, o, limit, kept_exps):
    length = q.shape[0]
    lane = lax.broadcasted_iota(jnp.int32, (length, PAIR), 1)
    live = lax.broadcasted_iota(jnp.int32, (length, PAIR), 0) < limit
    k_t = jnp.transpose(jnp.where(live, k, jnp.zeros_like(k)))
    inner = jnp.transpose(do.astype(f32) * o.astype(f32))
    dq_parts = []
    dk = jnp.zeros((length, PAIR), f32)
    dv = jnp.zeros((length, PAIR), f32)
    for h in range(2):
        keep = lane // HEAD_DIM == h
        v_h, do_h, q_h = [jnp.where(keep, m, jnp.zeros_like(m)) for m in (v, do, q)]
        exps = kept_exps(h)
        delta = jnp.sum(inner[h * HEAD_DIM : (h + 1) * HEAD_DIM], axis=0, keepdims=True)
        d_scores = (exps.astype(f32) * (dot_nt(v_h, do) - delta)).astype(bf16)
        dv = dv + dot_nn(exps, do_h)
        dk = dk + dot_nn(d_scores, q_h)
        dq_parts.append(dot_nn(k_t[h * HEAD_DIM : (h + 1) * HEAD_DIM], d_scores))
    dq = jnp.transpose(jnp.concatenate(dq_parts, axis=0)) * score_scale
    dk = jnp.where(live, dk * score_scale, 0.0)
    return dq.astype(bf16), dk.astype(bf16), dv.astype(bf16)


def own_lengths(short_ref, long_ref):
    s = lax.axis_index("seq")
    return long_ref[s // 2, 0, s % 2], short_ref[0, 0, s], short_ref[1, 0, s]


class Part:
    def __init__(self, own, out, sems, direct=False):
        self.own, self.out, self.direct = own, out, direct
        self.z_send, self.z_recv, self.x_send, self.x_recv, self.y_send, self.y_recv, self.c_send, self.c_recv = sems
        self.dp, self.s, self.z, self.x, self.y, self.c = place()
        self.rows, cols = own.shape
        self.half_rows, self.half_cols = self.rows // 2, cols // 2

    def cols(self, core):
        return pl.ds(pl.multiple_of(core * self.half_cols, 128), self.half_cols)

    def some(self, q):
        return pl.ds(pl.multiple_of(q * self.half_rows, 16), self.half_rows)

    def block(self, zs, x, core, q=None):
        rows = slice(None) if q is None else self.some(q)
        return self.out.at[zs * 2 + x, rows, self.cols(core)]

    def source(self, zs, own, q=None):
        if own:
            rows = slice(None) if q is None else self.some(q)
            return self.own.at[rows, self.cols(self.c)]
        return self.block(zs, self.x, self.c, q)

    def up(self, zs, own=False):
        dst = self.block(zs, self.x, self.c)
        return remote(self.source(zs, own), dst, self.z_send.at[zs, 0], self.z_recv.at[zs], (self.dp + 2, self.s))

    def down(self, zs, own=False):
        dst = self.block(zs, self.x, self.c)
        return remote(self.source(zs, own), dst, self.z_send.at[zs, 1], self.z_recv.at[zs], (self.dp - 2, self.s))

    def across(self, zs, own=False):
        q = None if self.direct else self.y
        dst = self.block(zs, self.x, self.c, q)
        device = (self.z * 2 + 1 - self.x, self.s)
        return remote(self.source(zs, own, q), dst, self.x_send.at[zs], self.x_recv.at[zs], device)

    def across_in(self, zs):
        ref = self.block(zs, 1 - self.x, self.c, None if self.direct else self.y)
        return remote(ref, ref, self.x_send.at[zs], self.x_recv.at[zs], (self.dp, self.s))

    def over(self, zs):
        ref = self.block(zs, 1 - self.x, self.c, self.y)
        return remote(ref, ref, self.y_send.at[zs], self.y_recv.at[zs], (self.dp, (1 - self.y) * 2 + self.c))

    def over_in(self, zs):
        ref = self.block(zs, 1 - self.x, self.c, 1 - self.y)
        return remote(ref, ref, self.y_send.at[zs], self.y_recv.at[zs], (self.dp, self.s))

    def share(self, kind, zs, core):
        if kind == 0:
            ref = self.block(zs, self.x, core)
        else:
            q = self.y if kind == 1 else 1 - self.y
            ref = self.block(zs, 1 - self.x, core, None if self.direct else q)
        j = kind * Z_CHIPS + zs
        return remote(ref, ref, self.c_send.at[j], self.c_recv.at[j], (self.dp, self.s + 1 - 2 * self.c))

    def each(self, k, what):
        if k == 0:
            what(self.z)
            return

        @pl.when(self.z >= k)
        def _():
            what(self.z - k)

        @pl.when(self.z + k < Z_CHIPS)
        def _():
            what(self.z + k)

    def stage(self, k):
        if k == 0:

            @pl.when(self.z < Z_CHIPS - 1)
            def _():
                self.up(self.z, True).start()

            @pl.when(self.z > 0)
            def _():
                self.down(self.z, True).start()

            self.across(self.z, True).start()
        elif k < Z_CHIPS:

            @pl.when(self.z >= k)
            def _():
                zs = self.z - k
                self.up(zs).wait_recv()

                @pl.when(self.z < Z_CHIPS - 1)
                def _():
                    self.up(zs).start()

                self.across(zs).start()
                self.share(0, zs, self.c).start()

            @pl.when(self.z + k < Z_CHIPS)
            def _():
                zs = self.z + k
                self.down(zs).wait_recv()

                @pl.when(self.z > 0)
                def _():
                    self.down(zs).start()

                self.across(zs).start()
                self.share(0, zs, self.c).start()

        if 1 <= k <= Z_CHIPS:

            def pass_x(zs):
                self.across_in(zs).wait_recv()
                if not self.direct:
                    self.over(zs).start()
                self.share(1, zs, self.c).start()

            self.each(k - 1, pass_x)
        if 2 <= k <= Z_CHIPS + 1 and not self.direct:

            def pass_y(zs):
                self.over_in(zs).wait_recv()
                self.share(2, zs, self.c).start()

            self.each(k - 2, pass_y)

    stages = Z_CHIPS + 2

    def finish(self):
        for kind in range(2 if self.direct else 3):
            for k in range(1 if kind == 0 else 0, Z_CHIPS):
                self.each(k, lambda zs, kind=kind: self.share(kind, zs, 1 - self.c).wait_recv())

    def settle(self):
        for k in range(Z_CHIPS):

            @pl.when((self.z >= k) & (self.z < Z_CHIPS - 1))
            def _():
                self.up(self.z - k, k == 0).wait_send()

            @pl.when((self.z + k < Z_CHIPS) & (self.z > 0))
            def _():
                self.down(self.z + k, k == 0).wait_send()

            self.each(k, lambda zs, k=k: self.across(zs, k == 0).wait_send())
            if not self.direct:
                self.each(k, lambda zs: self.over(zs).wait_send())
            for kind in range(2 if self.direct else 3):
                if kind > 0 or k > 0:
                    self.each(k, lambda zs, kind=kind: self.share(kind, zs, self.c).wait_send())


class Tokens:
    def __init__(self, long_ref, short_ref, out, send, recv, local):
        self.long_ref, self.short_ref, self.out, self.send, self.recv, self.local = long_ref, short_ref, out, send, recv, local
        self.dp, self.s = lax.axis_index("dp"), lax.axis_index("seq")

    def pieces(self, target, source):
        yield self.long_ref.at[target // 2, target % 2], self.out.at[source, pl.ds(0, 128)]
        yield self.short_ref.at[0, target], self.out.at[source, pl.ds(128, 64)]
        yield self.short_ref.at[1, target], self.out.at[source, pl.ds(192, 64)]

    def copies(self, k):
        target = (self.s + k) % 4
        for j, (src, dst) in enumerate(self.pieces(target, self.s)):
            yield remote(src, dst, self.send.at[k, j], self.recv.at[k, j], (self.dp, target))

    def own(self):
        for j, (src, dst) in enumerate(self.pieces(self.s, self.s)):
            yield pltpu.make_async_copy(src, dst, self.local.at[j])

    def start(self):
        for k in range(1, 4):
            for copy in self.copies(k):
                copy.start()
        for copy in self.own():
            copy.start()

    def finish(self):
        for copy in self.own():
            copy.wait()
        for k in range(1, 4):
            source = (self.s + 4 - k) % 4
            for j, (src, dst) in enumerate(self.pieces(self.s, source)):
                remote(src, dst, self.send.at[k, j], self.recv.at[k, j], (self.dp, self.s)).wait_recv()

    def settle(self):
        for k in range(1, 4):
            for copy in self.copies(k):
                copy.wait_send()


def layer_norm_back(grad, normed, inverse):
    return inverse * (grad - row_mean(grad) - normed * row_mean(grad * normed))


def live_rows(r, lens_ref):
    j = lax.broadcasted_iota(jnp.int32, (256, 1), 0)
    ends = [lens_ref[0] - r * 128] + [lens_ref[i] - r * 64 + first for i, first in ((1, 128), (2, 192))]
    return j < jnp.where(j < 128, ends[0], jnp.where(j < 192, ends[1], ends[2]))


DIRECT = (False, False, False, True)
FIRST_JOBS = ((0, 1), (1, 0), (0, 2), (2, 0), (0, 3), (1, 1), (0, 4), (2, 1), (0, 5), (1, 2),)
PROJECT_JOBS = {
    5: ((2, 2),),
    7: ((1, 3),),
    8: ((3, 0),),
}
ATTENTION_JOBS = {
    1: ((2, 3),),
    2: ((1, 4),),
    3: ((3, 1), (1, 5), (2, 4), (4, 0),),
    5: ((2, 5),),
}
INNER_FIRST_JOBS = ((3, 2),)
INNER_JOBS = {
    2: ((3, 3),),
}
OUTER_FIRST_JOBS = ((3, 4),)


def forward_kernel(*refs):
    refs = list(refs)

    def take(n):
        out = refs[:n]
        del refs[:n]
        return out

    short_len_ref, long_len_ref, wide_hbm, down_hbm, vec_ref = take(5)
    long_in, short_in, long_cot, short_cot = take(4)
    qkv_w_out, wo_out, w1_out, w2_out, tok_out, qkv_out, att_out, probs_out = take(8)
    act_out, slope_out, y1b_out, norm_out, inv_out, dz_out, dfb_out, out_out = take(8)
    (ainv_out,) = take(1)
    vec_out, sums_out = take(2)
    own_wide, own_down, w_s, wo_s, w1_s, w2_s, x_s, cot_s, qkv_s, att_s, vec_s, bias_s = take(12)
    stage_s, act_s, y1_s, y1b_s, norm_s, inv_s, dfb_s, out_s = take(8)
    z_send, z_recv, x_send, x_recv, y_send, y_recv, c_send, c_recv, v_send, v_recv, t_send, t_recv = take(12)
    local, keep_sem, stage_sem = take(3)
    wide_ref, down_ref, state_sem, ainv_s = take(4)

    dp, s, z, x, y, c = place()
    lens_ref = own_lengths(short_len_ref, long_len_ref)
    ranges = ((0, 3 * D), (3 * D, D + FF))
    load_wide = [
        pltpu.make_async_copy(
            wide_hbm.at[:, pl.ds(first, cols)], wide_ref.at[:, pl.ds(first, cols)], state_sem.at[i]
        )
        for i, (first, cols) in enumerate(ranges)
    ]
    load_down = pltpu.make_async_copy(down_hbm, down_ref, state_sem.at[2])
    for copy in load_wide + [load_down]:
        copy.start()
    greet()
    tokens = Tokens(long_in, short_in, x_s, t_send.at[0], t_recv.at[0], local.at[0])
    cots = Tokens(long_cot, short_cot, cot_s, t_send.at[1], t_recv.at[1], local.at[1])
    tokens.start()
    load_wide[0].wait()
    own_wide[:, 0 : 3 * D] = wide_ref[:, 0 : 3 * D].astype(bf16)

    def vec_copy(k, source, target):
        return remote(vec_ref, vec_s.at[source], v_send.at[k], v_recv.at[k], (target, s))

    sems = lambda i: [
        r.at[i] for r in (z_send, z_recv, x_send, x_recv, y_send, y_recv, c_send, c_recv)
    ]
    owns = [own_wide.at[:, pl.ds(first, cols)] for first, cols in ((0, 3 * D), (3 * D, D), (4 * D, FF))] + [own_down]
    parts = [
        Part(own, out, sems(i), direct=DIRECT[i]) for i, (own, out) in enumerate(zip(owns, (w_s, wo_s, w1_s, w2_s)))
    ]

    def run(jobs):
        for index, stage in jobs:
            if index == len(parts):
                cots.start()
            else:
                parts[index].stage(stage)

    first = parts[0]
    first.stage(0)
    load_wide[1].wait()
    load_down.wait()
    for k in range(1, 8):
        vec_copy(k, dp, (dp + k) % 8).start()
    own_wide[:, 3 * D :] = wide_ref[:, 3 * D :].astype(bf16)
    own_down[...] = down_ref[...].astype(bf16)
    own_copies = [
        pltpu.make_async_copy(part.own, part.out.at[dp], local.at[2, i]) for i, part in enumerate(parts)
    ]
    own_copies.append(pltpu.make_async_copy(vec_ref, vec_s.at[dp], local.at[2, 4]))
    for copy in own_copies:
        copy.start()
    run(FIRST_JOBS)
    for copy in own_copies:
        copy.wait()
    for k in range(1, 8):
        vec_copy(k, (dp + 8 - k) % 8, dp).wait_recv()
    vec = vec_s[0].astype(f32)
    for d in range(1, 8):
        vec = vec + vec_s[d].astype(f32)
    vec_out[...] = vec
    bias_s[:, 0:D] = jnp.broadcast_to(vec[0:1, :], (8, D))
    bias_s[:, D : 2 * D] = jnp.zeros((8, D), f32)
    bias_s[:, 2 * D : 3 * D] = jnp.broadcast_to(vec[1:2, :], (8, D))
    sums_out[...] = jnp.zeros_like(sums_out)
    tokens.finish()
    first.finish()
    kept = []

    def keep(src, dst):
        copy = pltpu.make_async_copy(src, dst, keep_sem.at[len(kept)])
        copy.start()
        kept.append(copy)

    keep(x_s, tok_out)
    keep(w_s, qkv_w_out)

    def during(i, plan):
        for when, jobs in plan.items():

            @pl.when(i == when)
            def _():
                run(jobs)

    def project(j, carry):
        during(j, PROJECT_JOBS)
        cols = pl.ds(pl.multiple_of(j * 256, 256), 256)
        w = w_s[:, :, cols].reshape(D, 256)
        rows = x_s[...].reshape(1024, D)
        qkv_s[:, :, cols] = (dot_nn(rows, w) + bias_s[0:1, cols]).astype(bf16).reshape(4, 256, 256)
        return carry

    lax.fori_loop(0, 3 * D // 256, project, 0)
    keep(qkv_s, qkv_out)
    pairs = D // PAIR

    def probs_copy(i, slot):
        return pltpu.make_async_copy(stage_s.at[slot], probs_out.at[i], stage_sem.at[slot])

    def attention(i, carry):
        during(i, ATTENTION_JOBS)
        slot = i % 2

        @pl.when(i >= 2)
        def _():
            probs_copy(i - 2, slot).wait()

        lanes = pl.ds(pl.multiple_of(i * PAIR, PAIR), PAIR)
        for first_row, rows, length, index in SEQS:
            q, k, v = [
                qkv_s[:, first_row : first_row + rows, pl.ds(pl.multiple_of(base + i * PAIR, PAIR), PAIR)].reshape(
                    length, PAIR
                )
                for base in (0, D, 2 * D)
            ]

            def keep_probs(h, probs, index=index):
                if index == 0:
                    stage_s[slot, h * LONG_L : (h + 1) * LONG_L, 0:LONG_L] = probs
                else:
                    row = (2 * h + index - 1) * SHORT_L
                    stage_s[slot, row : row + SHORT_L, LONG_L : LONG_L + SHORT_L] = probs

            o, inverse = attend_sums(q, k, v, lens_ref[index], keep_probs)
            att_s[:, first_row : first_row + rows, lanes] = o.reshape(4, rows, PAIR)
            ainv_s[:, first_row : first_row + rows, lanes] = inverse.reshape(4, rows, PAIR)
        probs_copy(i, slot).start()
        return carry

    lax.fori_loop(0, pairs, attention, 0)
    keep(att_s, att_out)
    keep(ainv_s, ainv_out)
    run(INNER_FIRST_JOBS)
    parts[1].finish()
    parts[2].finish()
    keep(wo_s, wo_out)
    keep(w1_s, w1_out)
    row_vec = lambda i: vec_out[i : i + 1, :]

    def slope_copy(r, slot):
        return pltpu.make_async_copy(stage_s.at[slot], slope_out.at[r], stage_sem.at[slot])

    def inner(r, carry):
        during(r, INNER_JOBS)
        slot = r % 2

        @pl.when(r < 2)
        def _():
            probs_copy(pairs - 2 + r, slot).wait()

        @pl.when(r >= 2)
        def _():
            slope_copy(r - 2, slot).wait()

        h = x_s[r].astype(f32) + (dot_nn(att_s[r], wo_s[...].reshape(D, D)) + row_vec(2))
        centred = h - row_mean(h)
        inverse = lax.rsqrt(row_mean(centred * centred) + norm_eps)
        normed = centred * inverse
        y1 = normed * row_vec(3) + row_vec(4)
        y1b = y1.astype(bf16)
        y1_s[r] = y1
        y1b_s[r] = y1b
        norm_s[r] = normed.astype(bf16)
        inv_s[r] = jnp.broadcast_to(inverse, (256, 128))
        at = pl.ds(pl.multiple_of(r * 256, 256), 256)
        for k in range(FF // D):
            w = w1_s[:, :, k * D : (k + 1) * D].reshape(D, D)
            act, slope = gelu_pair(dot_nn(y1b, w) + row_vec(8 + k))
            act_s[k, at] = act.astype(bf16)
            stage_s[slot, k * 256 : (k + 1) * 256] = slope.astype(bf16)
        slope_copy(r, slot).start()
        return carry

    lax.fori_loop(0, 4, inner, 0)
    for src, dst in ((act_s, act_out), (y1b_s, y1b_out), (norm_s, norm_out), (inv_s, inv_out)):
        keep(src, dst)
    run(OUTER_FIRST_JOBS)
    parts[3].finish()
    keep(w2_s, w2_out)
    cots.finish()

    def outer(r, carry):
        at = pl.ds(pl.multiple_of(r * 256, 256), 256)
        total = y1_s[r] + row_vec(5)
        for k in range(FF // D):
            total = total + dot_nn(act_s[k, at], w2_s[2 * k : 2 * k + 2].reshape(D, D))
        centred = total - row_mean(total)
        inverse = lax.rsqrt(row_mean(centred * centred) + norm_eps)
        normed = centred * inverse
        out_s[r] = (normed * row_vec(6) + row_vec(7)).astype(bf16)
        dr = jnp.where(live_rows(r, lens_ref), cot_s[r].astype(f32), 0.0)
        dz = layer_norm_back(dr * row_vec(6), normed, inverse)
        dfb = dz.astype(bf16)
        y1_s[r] = dz
        dfb_s[r] = dfb
        for i, v in ((5, dfb.astype(f32)), (6, dr * normed), (7, dr)):
            sums_out[i : i + 1, :] += jnp.sum(v, axis=0, keepdims=True)
        return carry

    lax.fori_loop(0, 4, outer, 0)
    for src, dst in ((y1_s, dz_out), (dfb_s, dfb_out), (out_s, out_out)):
        keep(src, dst)
    for copy in kept:
        copy.wait()
    for r in (2, 3):
        slope_copy(r, r % 2).wait()
    for k in range(1, 8):
        vec_copy(k, dp, (dp + k) % 8).wait_send()
    for part in parts:
        part.settle()
    tokens.settle()
    cots.settle()


def forward(short_len, long_len, wide_master, down_master, vec_block, long_in, short_in, long_cot, short_cot):
    any_spec = pl.BlockSpec(memory_space=pl.ANY)
    vmem = pl.BlockSpec(memory_space=pltpu.VMEM)
    smem = pl.BlockSpec(memory_space=pltpu.SMEM)
    shape = jax.ShapeDtypeStruct
    rows, down_rows = wide_master.shape[0], down_master.shape[0]
    dma = pltpu.SemaphoreType.DMA
    tok = (4, 256, D)
    outs = [
        ((8, rows, 3 * D), bf16),
        ((8, rows, D), bf16),
        ((8, rows, FF), bf16),
        ((8, down_rows, D), bf16),
        (tok, bf16),
        ((4, 256, 3 * D), bf16),
        (tok, bf16),
        ((D // PAIR, 1024, D), bf16),
        ((4, 1024, D), bf16),
        ((4, 1024, D), bf16),
        (tok, bf16),
        (tok, bf16),
        ((4, 256, 128), f32),
        (tok, f32),
        (tok, bf16),
        (tok, bf16),
        (tok, f32),
    ]
    vm = lambda dims, t=bf16: pltpu.VMEM(dims, t)
    return pl.pallas_call(
        forward_kernel,
        in_specs=[smem, smem, any_spec, any_spec, vmem] + [any_spec] * 4,
        out_specs=[any_spec] * len(outs) + [vmem] * 2,
        out_shape=[shape(dims, t) for dims, t in outs] + [shape((16, D), f32)] * 2,
        scratch_shapes=[
            vm((rows, 4 * D + FF)),
            vm((down_rows, D)),
            vm((8, rows, 3 * D)),
            vm((8, rows, D)),
            vm((8, rows, FF)),
            vm((8, down_rows, D)),
            vm(tok),
            vm(tok),
            vm((4, 256, 3 * D)),
            vm(tok),
            vm((8, 16, D)),
            vm((8, 3 * D), f32),
            vm((2, 1024, D)),
            vm((4, 1024, D)),
            vm(tok, f32),
            vm(tok),
            vm(tok),
            vm((4, 256, 128), f32),
            vm(tok),
            vm(tok),
            dma((4, 4, 2)),
            dma((4, 4)),
            dma((4, 4)),
            dma((4, 4)),
            dma((4, 4)),
            dma((4, 4)),
            dma((4, 12)),
            dma((4, 12)),
            dma((8,)),
            dma((8,)),
            dma((2, 4, 3)),
            dma((2, 4, 3)),
            dma((3, 5)),
            dma((16,)),
            dma((2,)),
            vm((rows, 4 * D + FF), f32),
            vm((down_rows, D), f32),
            dma((3,)),
            vm(tok, f32),
        ],
        compiler_params=pltpu.CompilerParams(
            vmem_limit_bytes=VMEM_BYTES, collective_id=0, has_side_effects=True
        ),
        name="forward",
    )(short_len, long_len, wide_master, down_master, vec_block, long_in, short_in, long_cot, short_cot)


class Grad:
    def __init__(self, theirs, acc, cbuf, xbuf, ybuf, zbuf, quarter, fin, sems, order):
        self.theirs, self.acc, self.cbuf, self.xbuf, self.ybuf, self.zbuf = theirs, acc, cbuf, xbuf, ybuf, zbuf
        self.quarter, self.fin, self.order = quarter, fin, order
        self.c_send, self.c_recv, self.x_send, self.x_recv, self.y_send, self.y_recv = sems[:6]
        self.z_send, self.z_recv, self.f_send, self.f_recv, self.local = sems[6:]
        self.dp, self.s, self.z, self.x, self.y, self.c = place()
        self.rows, cols = fin.shape
        self.half_rows, self.half_cols = self.rows // 2, cols // 2
        self.by_z = self.rows == 384
        self.core_pieces = 4 if self.by_z else 2
        self.mine = self.some(self.y)

    def cols(self, core):
        return pl.ds(pl.multiple_of(core * self.half_cols, 128), self.half_cols)

    def some(self, q):
        return pl.ds(pl.multiple_of(q * self.half_rows, 16), self.half_rows)

    def core_view(self, ref, j):
        if self.by_z:
            return ref.at[j]
        if self.order[0] != "y":
            return ref.at[:, (1 - self.x) if j == 0 else self.x]
        return ref.at[:, :, self.some((1 - self.y) if j == 0 else self.y)]

    def core_copy(self, j):
        return remote(
            self.core_view(self.theirs, j),
            self.core_view(self.cbuf, j),
            self.c_send.at[j],
            self.c_recv.at[j],
            (self.dp, self.s + 1 - 2 * self.c),
        )

    def x_copy(self, zd):
        device = (self.z * 2 + 1 - self.x, self.s)
        j = 0 if self.order == "zxy" else zd
        src = self.acc.at[zd, 1 - self.x, self.mine] if self.order == "yxz" else self.acc.at[zd, 1 - self.x]
        return remote(src, self.xbuf.at[j], self.x_send.at[j], self.x_recv.at[j], device)

    def y_copy(self, zd):
        device = (self.dp, (1 - self.y) * 2 + self.c)
        j = 0 if self.order[2] == "y" else zd
        rows = self.some(1 - self.y)
        src = self.acc.at[zd, :, rows] if self.order == "yxz" else self.acc.at[zd, self.x, rows]
        return remote(src, self.ybuf.at[j], self.y_send.at[j], self.y_recv.at[j], device)

    def z_copy(self, k):
        zd = (self.z + k) % Z_CHIPS
        src = self.acc.at[zd, self.x, self.mine]
        if self.order == "zxy":
            src = self.acc.at[zd]
        elif self.order == "xzy":
            src = self.acc.at[zd, self.x]
        return remote(
            src, self.zbuf.at[k - 1], self.z_send.at[k], self.z_recv.at[k], (zd * 2 + self.x, self.s)
        )

    def fin_quarter(self, y, core):
        return self.fin.at[self.some(y), self.cols(core)]

    def fin_copy(self, k):
        device = (self.dp, (1 - self.y) * 2 + self.c) if k == 2 else (self.dp, self.s + 1 - 2 * self.c)
        y = 1 - self.y if k == 3 else self.y
        dst = self.fin_quarter(y, self.c)
        return remote(dst if k == 3 else self.quarter, dst, self.f_send.at[k], self.f_recv.at[k], device)

    def fin_in(self, k):
        ref = self.fin_quarter(self.y if k == 1 else 1 - self.y, self.c if k == 2 else 1 - self.c)
        return remote(self.quarter, ref, self.f_send.at[k], self.f_recv.at[k], (self.dp, self.s))

    def fin_own(self):
        return pltpu.make_async_copy(self.quarter, self.fin_quarter(self.y, self.c), self.local)

    def core_start(self):
        for j in range(self.core_pieces):
            self.core_copy(j).start()

    def core_sent(self):
        for j in range(self.core_pieces):
            self.core_copy(j).wait_send()

    def z_block(self, k):
        zd = (self.z + k) % Z_CHIPS
        self.core_copy(zd).wait_recv()
        for xd in range(2):
            self.acc[zd, xd] = (self.acc[zd, xd].astype(f32) + self.cbuf[zd, xd].astype(f32)).astype(bf16)
        if self.order[0] == "x":
            self.x_copy(zd).start()
        elif k % Z_CHIPS:
            self.z_copy(k % Z_CHIPS).start()

    def core_add(self, j):
        self.core_copy(j).wait_recv()
        if self.order[0] != "y":
            xd = (1 - self.x) if j == 0 else self.x

            def one(zd, carry):
                self.acc[zd, xd] = (self.acc[zd, xd].astype(f32) + self.cbuf[zd, xd].astype(f32)).astype(bf16)
                return carry

        else:
            rows = self.some((1 - self.y) if j == 0 else self.y)

            def one(zd, carry):
                for xd in range(2):
                    self.acc[zd, xd, rows] = (
                        self.acc[zd, xd, rows].astype(f32) + self.cbuf[zd, xd, rows].astype(f32)
                    ).astype(bf16)
                return carry

        lax.fori_loop(0, Z_CHIPS, one, 0)

    def second(self, k):
        zd = (self.z + k + 1) % Z_CHIPS
        if self.order[0] == "x":
            self.x_copy(zd).wait_recv()
            self.acc[zd, self.x] = (self.acc[zd, self.x].astype(f32) + self.xbuf[zd].astype(f32)).astype(bf16)
            if self.order == "xyz":
                self.y_copy(zd).start()
            elif k < 3:
                self.z_copy(k + 1).start()
        else:
            self.y_copy(zd).wait_recv()
            for xd in range(2):
                self.acc[zd, xd, self.mine] = (
                    self.acc[zd, xd, self.mine].astype(f32) + self.ybuf[zd, xd].astype(f32)
                ).astype(bf16)
            self.x_copy(zd).start()

    def third(self, k):
        zd = (self.z + k) % Z_CHIPS
        if self.order == "xyz":
            self.y_copy(zd).wait_recv()
            came = self.ybuf
        else:
            self.x_copy(zd).wait_recv()
            came = self.xbuf
        self.acc[zd, self.x, self.mine] = (
            self.acc[zd, self.x, self.mine].astype(f32) + came[zd].astype(f32)
        ).astype(bf16)
        if k:
            self.z_copy(k).start()

    def publish(self, total):
        self.quarter[...] = total.astype(bf16)
        self.fin_own().start()
        self.fin_copy(1).start()
        self.fin_copy(2).start()

    def stage(self, i):
        if i >= 40:
            self.third((i - 39) % Z_CHIPS)
        elif i >= 30:
            self.second(i - 30)
        elif i == 6:
            self.fin_in(2).wait_recv()
            self.fin_copy(3).start()
        elif i == 7:
            self.fin_own().wait()
            self.fin_in(1).wait_recv()
            self.fin_in(3).wait_recv()
        elif self.order != "zxy":
            if i == 1:
                self.core_add(0)
                for k in range(Z_CHIPS):
                    zd = (self.z + k + 1) % Z_CHIPS
                    (self.x_copy(zd) if self.order[0] == "x" else self.y_copy(zd)).start()
            elif i == 2:
                self.core_add(1)
            elif i == 3:
                for k in range(Z_CHIPS):
                    self.second(k)
            elif i == 4 and self.order == "xzy":
                total = self.acc[self.z, self.x].astype(f32)
                for k in range(1, Z_CHIPS):
                    self.z_copy(k).wait_recv()
                    total = total + self.zbuf[k - 1].astype(f32)
                self.acc[self.z, self.x] = total.astype(bf16)
                self.y_copy(self.z).start()
            elif i == 4:
                for k in (1, 2, 3, 0):
                    self.third(k)
            elif i == 5 and self.order == "xzy":
                self.y_copy(self.z).wait_recv()
                self.publish(self.acc[self.z, self.x, self.mine].astype(f32) + self.ybuf[0].astype(f32))
            elif i == 5:
                total = self.acc[self.z, self.x, self.mine].astype(f32)
                for k in range(1, Z_CHIPS):
                    self.z_copy(k).wait_recv()
                    total = total + self.zbuf[k - 1].astype(f32)
                self.publish(total)
        else:
            if i == 1:
                self.core_add(0)
            elif i == 2:
                self.core_add(1)
                for k in range(1, Z_CHIPS):
                    self.z_copy(k).start()
            elif i == 3:
                for k in range(1, Z_CHIPS):
                    self.z_copy(k).wait_recv()
                for xd in range(2):
                    total = self.acc[self.z, xd].astype(f32)
                    for k in range(1, Z_CHIPS):
                        total = total + self.zbuf[k - 1, xd].astype(f32)
                    self.acc[self.z, xd] = total.astype(bf16)
                self.x_copy(self.z).start()
            elif i == 4:
                self.x_copy(self.z).wait_recv()
                total = self.acc[self.z, self.x].astype(f32) + self.xbuf[0].astype(f32)
                self.acc[self.z, self.x] = total.astype(bf16)
                self.y_copy(self.z).start()
            elif i == 5:
                self.y_copy(self.z).wait_recv()
                self.publish(self.acc[self.z, self.x, self.mine].astype(f32) + self.ybuf[0].astype(f32))

    def settle(self):
        for k in range(1, Z_CHIPS):
            self.z_copy(k).wait_send()
        for k in range(1, 4):
            self.fin_copy(k).wait_send()
        for k in range(1 if self.order == "zxy" else Z_CHIPS):
            self.x_copy((self.z + k) % Z_CHIPS).wait_send()
        for k in range(1 if self.order[2] == "y" else Z_CHIPS):
            self.y_copy((self.z + k) % Z_CHIPS).wait_send()


class Returns:
    def __init__(self, rows_ref, long_out, short_out, send, recv, local, own_rows=None):
        self.rows_ref, self.long_out, self.short_out = rows_ref, long_out, short_out
        self.send, self.recv, self.local = send, recv, local
        self.dp, self.s = lax.axis_index("dp"), lax.axis_index("seq")
        self.own_rows = rows_ref.at[self.s] if own_rows is None else own_rows

    def own(self):
        for j, (first, rows, (_, dst)) in enumerate(zip((0, 128, 192), (128, 64, 64), self.pieces(self.s, self.s))):
            yield pltpu.make_async_copy(self.own_rows.at[pl.ds(first, rows)], dst, self.local.at[j])

    def pieces(self, target, source):
        yield self.rows_ref.at[target, pl.ds(0, 128)], self.long_out.at[source // 2, source % 2]
        yield self.rows_ref.at[target, pl.ds(128, 64)], self.short_out.at[0, source]
        yield self.rows_ref.at[target, pl.ds(192, 64)], self.short_out.at[1, source]

    copies, start, finish, settle = Tokens.copies, Tokens.start, Tokens.finish, Tokens.settle


def sums_window(d):
    return jnp.minimum(d * 96 // 128, 4) * 128


class Sums:
    def __init__(self, src, sbuf, part, dbuf, out, sems):
        self.src, self.sbuf, self.part, self.dbuf, self.out = src, sbuf, part, dbuf, out
        self.s_send, self.s_recv, self.d_send, self.d_recv = sems
        self.dp, self.s = lax.axis_index("dp"), lax.axis_index("seq")

    def s_copy(self, k, source):
        return remote(self.src, self.sbuf.at[source], self.s_send.at[k], self.s_recv.at[k], (self.dp, (self.s + k) % 4))

    def window(self, d):
        return self.part.at[:, pl.ds(pl.multiple_of(sums_window(d), 128), 256)]

    def d_copy(self, k, source):
        target = (self.dp + k) % 8
        return remote(self.window(target), self.dbuf.at[source], self.d_send.at[k], self.d_recv.at[k], (target, self.s))

    def stage(self, i):
        if i == 0:
            for k in range(1, 4):
                self.s_copy(k, self.s).start()
            self.sbuf[self.s] = self.src[...]
        elif i == 1:
            for k in range(1, 4):
                self.s_copy(k, (self.s + 4 - k) % 4).wait_recv()
            self.part[...] = (self.sbuf[0] + self.sbuf[1]) + (self.sbuf[2] + self.sbuf[3])
            for k in range(1, 8):
                self.d_copy(k, self.dp).start()
            self.dbuf[self.dp] = self.window(self.dp)[...]
        elif i == 2:
            for k in range(1, 8):
                self.d_copy(k, (self.dp + 8 - k) % 8).wait_recv()
            total = self.dbuf[0]
            for d in range(1, 8):
                total = total + self.dbuf[d]
            self.out[...] = total

    def settle(self):
        for k in range(1, 4):
            self.s_copy(k, self.s).wait_send()
        for k in range(1, 8):
            self.d_copy(k, self.dp).wait_send()


PIECES = (
    (384, D, "xzy"),
    (192, D, "yxz"),
    (192, D, "xyz"),
    (96, D, "xzy"),
    (96, D, "xzy"),
    (96, D, "xzy"),
    (96, D, "xzy"),
)


MIDDLE_JOBS = {
    0: (),
    1: ((0, 30),),
    2: ((0, 31),),
    3: (),
}
ONE_JOBS = ((2, 1),)
O_JOBS = ((1, 1),)
BEFORE_PAIR = {
    0: (),
    1: (),
    2: ((3, 1), (1, 2), (3, 2), (0, 32), (1, 30), (2, 2), (0, 33),),
    3: ((1, 31), (4, 1),),
    4: ((3, 31), (2, 30), (5, 1), (1, 33), (1, 40), (5, 2), (1, 41), (4, 30), (2, 31),),
    5: ((2, 32), (2, 33), (5, 30), (2, 40), (5, 31), (0, 5),),
}
AFTER_GROUP = (
    (),
    ((4, 2), (0, 4), (3, 30), (1, 32),),
    ((5, 32), (2, 41), (4, 31), (3, 32), (5, 33), (6, 1), (6, 2), (4, 32), (3, 33), (4, 33), (5, 4), (6, 30), (1, 42), (4, 4), (6, 31), (3, 4), (1, 43), (6, 32), (2, 42), (0, 6), (5, 5), (2, 43), (1, 5), (4, 5), (5, 6), (6, 33), (3, 5), (6, 4),),
)
LAST_JOBS = ((1, 6), (2, 5), (3, 6), (6, 5), (2, 6), (4, 6), (6, 6),)


def backward_kernel(*refs):
    refs = list(refs)

    def take(n):
        out = refs[:n]
        del refs[:n]
        return out

    short_len_ref, long_len_ref, vec_ref, sums_in = take(4)
    act_hbm, slope_hbm, y1b_hbm, norm_hbm, inv_hbm, ainv_hbm, dz_hbm, dfb_hbm, att_hbm, qkv_hbm, probs_hbm = take(11)
    tok_hbm, w_hbm, wo_hbm, w1_hbm, w2_hbm, out_rows = take(6)
    fins = take(len(PIECES))
    (sums_out,) = take(1)
    short_out, long_out, short_back, long_back = take(4)
    (theirs_a,) = take(1)
    bufs = [take(6) for _ in PIECES]
    big, dfb_s, y1b_s, att_s, at_s, first_s, second_s, wo_s, dub_s, dh_s, dob_s, inv_s, dqkv_s = take(13)
    sums_s, sbuf, part, dbuf = take(4)
    sems = take(11)
    s_sems = take(4)
    t_send, t_recv, local, load_sem, big_sem, ainv_s, ainv_sem, out_s = take(8)

    dp, s, z, x, y, c = place()
    lens_ref = own_lengths(short_len_ref, long_len_ref)
    greet()
    outs = Returns(out_rows, long_out, short_out, t_send.at[0], t_recv.at[0], local.at[0], out_s)
    backs = Returns(y1b_s, long_back, short_back, t_send.at[1], t_recv.at[1], local.at[1])

    def plan(i, *pairs):
        return [pltpu.make_async_copy(src, dst, load_sem.at[i + j]) for j, (src, dst) in enumerate(pairs)]

    def begin(copies):
        for copy in copies:
            copy.start()
        return copies

    def load(i, *pairs):
        return begin(plan(i, *pairs))

    def done(copies):
        for copy in copies:
            copy.wait()

    def big_copy(src, slot):
        return pltpu.make_async_copy(src, big.at[slot], big_sem.at[slot])

    def act_chunk(k):
        return act_hbm.at[(z + k) % Z_CHIPS]

    chunk = lambda i: pl.ds(i * D, D)
    big_copy(act_chunk(1), 1).start()
    load_dfb = load(0, (dfb_hbm, dfb_s))
    load_out = load(12, (out_rows.at[s], out_s))
    load_w2 = plan(1, (w2_hbm, second_s))
    load_w1 = plan(2, *[(w1_hbm.at[:, chunk(k)], first_s.at[chunk(k)]) for k in range(4)])
    load_mid = plan(6, (dz_hbm, dh_s), (norm_hbm, dob_s), (inv_hbm, inv_s), (wo_hbm, wo_s))
    load_y1b = plan(10, (y1b_hbm, y1b_s))
    load_att = plan(11, (att_hbm, att_s))

    pieces = []
    for i, (rows, cols, order) in enumerate(PIECES):
        first = (0, 0, 192, 0, 96, 192, 288)[i]
        theirs = theirs_a.at[:, :, pl.ds(first, rows), :]
        pieces.append(Grad(theirs, *bufs[i], fins[i], [r.at[i] for r in sems], order))
    down, one_a, one_b, o_piece = pieces[:4]
    sums = Sums(sums_s, sbuf, part, dbuf, sums_out, s_sems)
    done(load_out)
    outs.start()

    def run(jobs):
        for index, stage in jobs:
            pieces[index].stage(stage)

    def during(i, plan):
        for when, jobs in plan.items():

            @pl.when(i == when)
            def _():
                run(jobs)

    def columns(core):
        return pl.ds(pl.multiple_of(core * (D // 2), 128), D // 2)

    sums_s[...] = sums_in[...]
    done(load_dfb)

    def down_block(k, carry):
        zd = (z + k) % Z_CHIPS
        slot = k % 2
        big_copy(act_chunk(k), slot).wait()

        @pl.when(k < Z_CHIPS)
        def _():
            big_copy(act_chunk(k + 1), 1 - slot).start()

        @pl.when(k == Z_CHIPS)
        def _():
            big_copy(slope_hbm.at[0], 1 - slot).start()

        for j, later in ((1, load_w2), (2, load_w1), (3, load_mid), (4, load_y1b + load_att)):

            @pl.when(k == j)
            def _():
                begin(later)

        at_s[...] = jnp.transpose(big[slot])
        theirs_a[zd] = dot_nn(at_s[...], dfb_s[:, :, columns(1 - c)].reshape(1024, D // 2)).astype(bf16).reshape(2, 384, D // 2)
        down.core_copy(zd).start()
        down.acc[zd] = dot_nn(at_s[...], dfb_s[:, :, columns(c)].reshape(1024, D // 2)).astype(bf16).reshape(2, 384, D // 2)
        for j in range(2, Z_CHIPS + 1):

            @pl.when(k == j)
            def _():
                down.z_block(j - 1)

        return carry

    def ainv_copy(r, slot):
        return pltpu.make_async_copy(ainv_hbm.at[r], ainv_s.at[slot], ainv_sem.at[slot])

    lax.fori_loop(1, Z_CHIPS + 1, down_block, 0)
    ainv_copy(0, 0).start()
    done(load_w2)
    done(load_w1)
    done(load_mid)
    row_vec = lambda i: vec_ref[i : i + 1, :]

    def add(index, v):
        sums_s[index : index + 1, :] += jnp.sum(v, axis=0, keepdims=True)

    def middle_back(r, carry):
        slot = (r + 1) % 2
        big_copy(slope_hbm.at[r], slot).wait()

        @pl.when(r < 3)
        def _():
            big_copy(slope_hbm.at[r + 1], 1 - slot).start()

        @pl.when(r == 0)
        def _():
            down.z_block(Z_CHIPS)

        during(r, MIDDLE_JOBS)
        ainv_copy(r, r % 2).wait()

        @pl.when(r < 3)
        def _():
            ainv_copy(r + 1, (r + 1) % 2).start()

        at = pl.ds(pl.multiple_of(r * 256, 256), 256)
        dfb = dfb_s[r]
        dy1 = dh_s[r]
        for k in range(FF // D):
            slope = big[slot, k * 256 : (k + 1) * 256].astype(f32)
            dub = (dot_nt(dfb, second_s[k * D : (k + 1) * D]) * slope).astype(bf16)
            dub_s[k, at] = dub
            add(8 + k, dub.astype(f32))
            dy1 = dy1 + dot_nt(dub, first_s[k * D : (k + 1) * D])
        normed = dob_s[r].astype(f32)
        add(3, dy1 * normed)
        add(4, dy1)
        dh = layer_norm_back(dy1 * row_vec(3), normed, inv_s[r][:, 0:1])
        dab = dh.astype(bf16)
        dh_s[r] = dh
        dfb_s[r] = dab
        add(2, dab.astype(f32))
        dob_s[r] = (dot_nt(dab, wo_s[...]) * ainv_s[r % 2]).astype(bf16)
        return carry

    lax.fori_loop(0, 4, middle_back, 0)
    qkv_loads = load(1, *[(qkv_hbm.at[:, :, chunk(j)], first_s.at[pl.ds(j * 1024, 1024)].reshape(4, 256, D)) for j in range(3)])
    w_loads = load(4, *[(w_hbm.at[:, chunk(j)], second_s.at[chunk(j)]) for j in range(3)])

    def probs_copy(i, slot):
        return big_copy(probs_hbm.at[i], slot)

    probs_copy(0, 0).start()

    done(load_y1b)
    at_s[...] = jnp.transpose(y1b_s[...].reshape(1024, D))
    load_tok = load(10, (tok_hbm, y1b_s))
    down.core_sent()

    def one_block(k, carry):
        core = jnp.where(k < 2, 1 - c, c)
        grad = dot_nn(at_s[...], dub_s[core * 2 + k % 2]).astype(bf16)
        for e in range(2):
            half = grad[:, e * (D // 2) : (e + 1) * (D // 2)].reshape(4, 2, 96, D // 2)
            rows = pl.ds(e * 96, 96)
            for j, ref in enumerate((one_a.theirs, one_b.theirs, one_a.acc, one_b.acc)):

                @pl.when(k == j)
                def _():
                    ref[:, :, rows, :] = half

        for j, piece in ((0, one_a), (1, one_b)):

            @pl.when(k == j)
            def _():
                piece.core_start()

        return carry

    lax.fori_loop(0, 4, one_block, 0)
    run(ONE_JOBS)
    one_a.core_sent()
    one_b.core_sent()

    def small_grad(piece, right):
        piece.theirs[...] = dot_nn(at_s[...], right(1 - c)).astype(bf16).reshape(4, 2, 96, D // 2)
        piece.core_start()
        piece.acc[...] = dot_nn(at_s[...], right(c)).astype(bf16).reshape(4, 2, 96, D // 2)

    done(load_att)
    at_s[...] = jnp.transpose(att_s[...].reshape(1024, D))
    small_grad(o_piece, lambda core: dfb_s[:, :, columns(core)].reshape(1024, D // 2))
    run(O_JOBS)

    done(load_tok)
    at_s[...] = jnp.transpose(y1b_s[...].reshape(1024, D))
    done(qkv_loads)
    done(w_loads)
    pairs = D // PAIR

    for g in range(3):

        def pair(i, carry, g=g):
            during(i, {j: BEFORE_PAIR[j] for j in (2 * g, 2 * g + 1)})
            slot = i % 2
            probs_copy(i, slot).wait()

            @pl.when(i + 1 < pairs)
            def _():
                probs_copy(i + 1, 1 - slot).start()

            lanes = pl.ds(pl.multiple_of(i * PAIR, PAIR), PAIR)
            sum_q = jnp.zeros((1, PAIR), f32)
            sum_v = jnp.zeros((1, PAIR), f32)
            for first, rows, length, index in SEQS:
                q, k, v = [
                    first_s[j * 1024 : (j + 1) * 1024, lanes].reshape(4, 256, PAIR)[:, first : first + rows].reshape(length, PAIR)
                    for j in range(3)
                ]
                do, o = [r[:, first : first + rows, lanes].reshape(length, PAIR) for r in (dob_s, att_s)]

                def kept(h, index=index):
                    if index == 0:
                        return big[slot, h * LONG_L : (h + 1) * LONG_L, 0:LONG_L]
                    row = (2 * h + index - 1) * SHORT_L
                    return big[slot, row : row + SHORT_L, LONG_L : LONG_L + SHORT_L]

                grads = attend_sums_back(q, k, v, do, o, lens_ref[index], kept)
                sum_q = sum_q + jnp.sum(grads[0].astype(f32), axis=0, keepdims=True)
                sum_v = sum_v + jnp.sum(grads[2].astype(f32), axis=0, keepdims=True)
                for j in range(3):
                    dst = pl.ds(pl.multiple_of(j * 256 + (i % 2) * PAIR, PAIR), PAIR)
                    dqkv_s[:, first : first + rows, dst] = grads[j].reshape(4, rows, PAIR)
            sums_s[0:1, lanes] = sum_q
            sums_s[1:2, lanes] = sum_v
            return carry

        lax.fori_loop(2 * g, 2 * g + 2, pair, 0)
        small_grad(pieces[4 + g], lambda core: dqkv_s[:, :, columns(core)].reshape(1024, D // 2))
        if g == 2:
            sums.stage(0)

        def rows_back(r, carry, g=g):
            total = dh_s[r]
            for j in range(3):
                total = total + dot_nt(
                    dqkv_s[r, :, j * 256 : (j + 1) * 256], second_s[j * D : (j + 1) * D, g * 256 : (g + 1) * 256]
                )
            if g < 2:
                dh_s[r] = total
            else:
                y1b_s[r] = total.astype(bf16)
            return carry

        if g == 2:
            lax.fori_loop(0, 4, rows_back, 0)
            backs.start()
            run(AFTER_GROUP[g])
        else:
            run(AFTER_GROUP[g])
            lax.fori_loop(0, 4, rows_back, 0)

    sums.stage(1)
    run(LAST_JOBS)
    sums.stage(2)
    run([(i, 7) for i in range(len(PIECES))])
    outs.finish()
    backs.finish()
    for i, piece in enumerate(pieces):
        if i > 2:
            piece.core_sent()
        piece.settle()
    sums.settle()
    outs.settle()
    backs.settle()


def backward(short_len, long_len, vec, sums, arrays, out_rows):
    any_spec = pl.BlockSpec(memory_space=pl.ANY)
    vmem = pl.BlockSpec(memory_space=pltpu.VMEM)
    smem = pl.BlockSpec(memory_space=pltpu.SMEM)
    shape = jax.ShapeDtypeStruct
    dma = pltpu.SemaphoreType.DMA
    count = len(PIECES)
    vm = lambda dims, t=bf16: pltpu.VMEM(dims, t)
    bufs = []
    for rows, cols, order in PIECES:
        half, cut = cols // 2, rows // 2
        bufs += [vm((4, 2, rows, half)), vm((4, 2, rows, half))]
        bufs += {
            "xyz": [vm((4, rows, half)), vm((4, cut, half)), vm((3, cut, half))],
            "yxz": [vm((4, cut, half)), vm((4, 2, cut, half)), vm((3, cut, half))],
            "xzy": [vm((4, rows, half)), vm((1, cut, half)), vm((3, rows, half))],
            "zxy": [vm((1, rows, half)), vm((1, cut, half)), vm((3, 2, rows, half))],
        }[order]
        bufs.append(vm((cut, half)))
    tok = (4, 256, D)
    return pl.pallas_call(
        backward_kernel,
        in_specs=[smem, smem, vmem, vmem] + [any_spec] * (len(arrays) + 1),
        out_specs=[any_spec] * count + [vmem] + [any_spec] * 4,
        out_shape=[shape((rows, cols), bf16) for rows, cols, _ in PIECES]
        + [
            shape((16, 256), f32),
            shape((2, 4, 64, D), bf16),
            shape((2, 2, 128, D), bf16),
            shape((2, 4, 64, D), bf16),
            shape((2, 2, 128, D), bf16),
        ],
        scratch_shapes=[vm((4, 2, 384, D // 2))]
        + bufs
        + [
            vm((2, 1024, D)),
            vm(tok),
            vm(tok),
            vm(tok),
            vm((D, 1024)),
            vm((FF, D)),
            vm((FF, D)),
            vm((D, D)),
            vm((4, 1024, D)),
            vm(tok, f32),
            vm(tok),
            vm((4, 256, 128), f32),
            vm(tok),
            vm((16, D), f32),
            vm((4, 16, D), f32),
            vm((16, D), f32),
            vm((8, 16, 256), f32),
        ]
        + [dma((count, 4))] * 10
        + [dma((count,))]
        + [dma((4,)), dma((4,)), dma((8,)), dma((8,))]
        + [dma((2, 4, 3)), dma((2, 4, 3)), dma((2, 3)), dma((13,)), dma((2,)), vm((2, 256, D), f32), dma((2,)), vm((256, D))],
        compiler_params=pltpu.CompilerParams(
            vmem_limit_bytes=VMEM_BYTES, collective_id=1, has_side_effects=True
        ),
        name="backward",
    )(short_len, long_len, vec, sums, *arrays, out_rows)


def transpose_dot(left, right):
    return jnp.einsum("ra,rb->ab", left, right, preferred_element_type=f32)


def right_dot(left, right):
    return jnp.einsum("ra,ba->rb", left, right, preferred_element_type=f32)


def flip(v, axis, bit):
    n = lax.axis_size(axis)
    return lax.ppermute(v, axis, [(i, i ^ bit) for i in range(n)])


def half_of(v, dim, which):
    size = v.shape[dim] // 2
    return lax.dynamic_slice_in_dim(v, which * size, size, dim)


def halve(v, axis, bit, dim):
    mine = (lax.axis_index(axis) // bit) % 2
    other = flip(half_of(v, dim, 1 - mine), axis, bit)
    return (half_of(v, dim, mine).astype(f32) + other.astype(f32)).astype(bf16)


def double(v, axis, bit, dim):
    mine = (lax.axis_index(axis) // bit) % 2
    other = flip(v, axis, bit)
    return jnp.where(
        mine == 0, jnp.concatenate([v, other], axis=dim), jnp.concatenate([other, v], axis=dim)
    )


def reduce_rows(grad):
    rows, cols = grad.shape
    dp = lax.axis_size("dp")
    v = grad.reshape(dp, rows // dp, cols)
    v = halve(v, "seq", 1, 2)
    v = halve(v, "seq", 2, 2)
    bit = 1
    while bit < dp:
        blocks = v.shape[0]
        v = v.reshape(blocks // 2, 2, v.shape[1], v.shape[2]) if v.ndim == 3 else v
        v = halve(v, "dp", bit, 1)[:, 0]
        bit *= 2
    v = v[0]
    v = double(v, "seq", 2, 1)
    v = double(v, "seq", 1, 1)
    return v.astype(f32)


def update(master, reduced_grad, moment, average):
    step_grad = reduced_grad + decay_weight * master
    velocity = momentum_rate * moment + step_grad
    updated = master - learning_rate * (step_grad + momentum_rate * velocity)
    averaged = average_rate * average + (1.0 - average_rate) * updated
    return (velocity, averaged, updated, updated.astype(jnp.bfloat16))


UPDATE_STEPS = 8


def update_kernel(*refs):
    refs = list(refs)

    def take(n):
        out = refs[:n]
        del refs[:n]
        return out

    down_low, one_a, one_b, o_low, low_0, low_1, low_2 = take(7)
    wide_state, down_state, passed = take(3), take(3), take(4)
    wide_out, down_out, passed_out = take(5), take(5), take(4)
    (grad_s,) = take(1)
    i = pl.program_id(0)
    for src, dst in zip(passed, passed_out):
        dst[...] = src[...]
    half = D // 2
    for b in range(UPDATE_STEPS):

        @pl.when(i == b)
        def _():
            if b < 3:
                for g, low in enumerate((low_0, low_1, low_2)):
                    grad_s[:, g * 256 : (g + 1) * 256] = low[:, b * 256 : (b + 1) * 256]
            elif b == 3:
                grad_s[...] = o_low[...]
            else:
                rows, core = grad_s.shape[0], (b - 4) // 2
                low = (one_a, one_b)[b % 2]
                for k in range(2):
                    part = low[k * rows : (k + 1) * rows, core * half : (core + 1) * half]
                    grad_s[:, k * half : (k + 1) * half] = part

    def step(grad, state, outs):
        master, moment, average = state
        outs[0][...] = grad
        for ref, v in zip(outs[1:], update(master[...], grad, moment[...], average[...])):
            ref[...] = v

    step(grad_s[...].astype(f32), wide_state, wide_out)
    rows = down_state[0].shape[0]
    step(down_low[pl.ds(pl.multiple_of(i * rows, 16), rows)].astype(f32), down_state, down_out)


def update_all(lows, wide, down, passed):
    rows, cols = wide[0].shape
    down_rows = down[0].shape[0]
    vmem = pl.BlockSpec(memory_space=pltpu.VMEM)
    short_spec = pl.BlockSpec((1, 1, 64, D), lambda i: (i // 4, i % 4, 0, 0))
    long_spec = pl.BlockSpec((1, 1, 64, D), lambda i: (i // 4, i % 4 // 2, i % 2, 0))
    passed_specs = [short_spec, long_spec, short_spec, long_spec]
    shape = jax.ShapeDtypeStruct
    wide_spec = pl.BlockSpec((rows, cols // UPDATE_STEPS), lambda i: (0, i))
    down_spec = pl.BlockSpec((down_rows // UPDATE_STEPS, D), lambda i: (i, 0))
    types = (f32, f32, f32, f32, bf16)
    return pl.pallas_call(
        update_kernel,
        grid=(UPDATE_STEPS,),
        in_specs=[vmem] * len(lows) + [wide_spec] * 3 + [down_spec] * 3 + passed_specs,
        out_specs=[wide_spec] * 5 + [down_spec] * 5 + passed_specs,
        out_shape=[shape((rows, cols), t) for t in types]
        + [shape((down_rows, D), t) for t in types]
        + [shape(p.shape, p.dtype) for p in passed],
        scratch_shapes=[pltpu.VMEM((rows, D), bf16)],
        compiler_params=params(),
        name="update",
    )(*lows, *wide, *down, *passed)


def spread_rows(long_part, short_part):
    long_blocks = long_part.reshape(4, 128, D)
    short_blocks = jnp.transpose(short_part, (1, 0, 2, 3)).reshape(4, 128, D)
    return jnp.concatenate([long_blocks, short_blocks], axis=1)


def exchange(v):
    return lax.all_to_all(v, "seq", split_axis=0, concat_axis=0, tiled=True)


def collect_rows(v):
    long_part = v[:, :128].reshape(2, 2, 128, D)
    short_part = jnp.transpose(v[:, 128:].reshape(4, 2, 64, D), (1, 0, 2, 3))
    return short_part, long_part


def body(
    short_in,
    long_in,
    short_cot,
    long_cot,
    short_len,
    long_len,
    wide_master,
    down_master,
    vector_master,
    wide_moment,
    down_moment,
    vector_moment,
    wide_average,
    down_average,
    vector_average,
):
    s = lax.axis_index("seq")
    own_rows = vector_master.shape[0]
    if lax.axis_size("dp") == 8:
        vec_own = jnp.pad(jnp.transpose(vector_master).astype(bf16), ((0, 4), (0, 0)))
        vec_block = lax.dynamic_update_slice(
            jnp.zeros((16, D), bf16), vec_own, (0, lax.axis_index("dp") * own_rows)
        )
        (w_qkv, w_o, w_1, w_2, tokens, qkv, attended, probs, act, slope, y1b, norm, inv, dz, dfb, out, att_inv, vec, sums) = forward(
            short_len, long_len, wide_master, down_master, vec_block, long_in, short_in, long_cot, short_cot
        )
        w_qkv, w_o, w_1, w_2 = [w.reshape(-1, w.shape[2]) for w in (w_qkv, w_o, w_1, w_2)]
        arrays = (act, slope, y1b, norm, inv, att_inv, dz, dfb, attended, qkv, probs, tokens, w_qkv, w_o, w_1, w_2)
        *lows, sums_own, short_out, long_out, short_back, long_back = backward(
            short_len, long_len, vec, sums, arrays, out
        )
        index = lax.axis_index("dp")
        own_sums = lax.dynamic_slice(sums_own, (0, index * own_rows - sums_window(index)), (12, own_rows))
        vector_reduced = jnp.transpose(own_sums)
        results = update_all(
            lows,
            (wide_master, wide_moment, wide_average),
            (down_master, down_moment, down_average),
            (short_out, long_out, short_back, long_back),
        )
        wide_reduced, *wide_new = results[:5]
        down_reduced, *down_new = results[5:10]
        short_out, long_out, short_back, long_back = results[10:]
    else:
        lens = jnp.stack([long_len[s // 2, 0, s % 2], short_len[0, 0, s], short_len[1, 0, s]])
        tokens = exchange(spread_rows(long_in, short_in))
        cotangent = exchange(spread_rows(long_cot, short_cot))
        wide_w = lax.all_gather(wide_master.astype(bf16), "dp", axis=0, tiled=True)
        w_2 = lax.all_gather(down_master.astype(bf16), "dp", axis=0, tiled=True)
        vector_w = lax.all_gather(vector_master.astype(bf16), "dp", axis=0, tiled=True)
        vec = jnp.transpose(vector_w.astype(f32))
        w_qkv = wide_w[:, : 3 * D]
        w_o = wide_w[:, 3 * D : 4 * D]
        w_1 = wide_w[:, 4 * D :]
        rows = tokens.reshape(1024, D)
        proj_bias = jnp.concatenate([vec[0], jnp.zeros((D,), f32), vec[1]])
        qkv = (jnp.dot(rows, w_qkv, preferred_element_type=f32) + proj_bias).astype(bf16)
        qkv = qkv.reshape(4, 256, 3 * D)
        attended, long_probs, short_probs = attn_forward(lens, qkv)
        flat_attended = attended.reshape(1024, D)
        out, y1b, act, dfb, dub, dab, dob, dh, sums = middle(
            lens, flat_attended, rows, cotangent.reshape(1024, D), w_o, w_1, w_2, vec
        )
        d_down = transpose_dot(act, dfb).astype(bf16)
        d_one = transpose_dot(y1b, dub).astype(bf16)
        d_o = transpose_dot(flat_attended, dab).astype(bf16)
        dq, dk, dv, qv_sums = attn_backward(
            lens, qkv, dob.reshape(4, 256, D), attended, long_probs, short_probs
        )
        d_qkv = jnp.concatenate([dq, dk, dv], axis=2).reshape(1024, 3 * D)
        d_wqkv = transpose_dot(rows, d_qkv).astype(bf16)
        back = (dh + right_dot(d_qkv, w_qkv)).astype(bf16).reshape(4, 256, D)
        vector_total = jnp.concatenate([qv_sums[:2], sums[2:12]], axis=0)
        vector_sum = jnp.transpose(lax.psum(vector_total, ("dp", "seq")))
        vector_reduced = lax.dynamic_slice_in_dim(vector_sum, lax.axis_index("dp") * own_rows, own_rows, 0)
        wide_reduced = jnp.concatenate([reduce_rows(d_wqkv), reduce_rows(d_o), reduce_rows(d_one)], axis=1)
        down_reduced = reduce_rows(d_down)
        short_out, long_out = collect_rows(exchange(out.reshape(4, 256, D)))
        short_back, long_back = collect_rows(exchange(back))
        wide_new = update(wide_master, wide_reduced, wide_moment, wide_average)
        down_new = update(down_master, down_reduced, down_moment, down_average)
    vector_new = update(vector_master, vector_reduced, vector_moment, vector_average)
    return (
        short_out,
        long_out,
        short_back,
        long_back,
        wide_reduced,
        down_reduced,
        vector_reduced,
        wide_new[0],
        down_new[0],
        vector_new[0],
        wide_new[1],
        down_new[1],
        vector_new[1],
        wide_new[2],
        down_new[2],
        vector_new[2],
        wide_new[3],
        down_new[3],
        vector_new[3],
    )


def solution(mesh):
    tok = P(None, "dp", "seq", None)
    lengths = P(None, "dp", None)
    state = P("dp", None)
    return jax.shard_map(
        body,
        mesh=mesh,
        in_specs=(tok,) * 4 + (lengths,) * 2 + (state,) * 9,
        out_specs=(tok,) * 4 + (state,) * 15,
        check_vma=False,
    )
```

profile of v0, /device:TPU:0, one launch (start us, length us, event | category | flops | bytes accessed | tf_op | source)
XLA Modules:
  0.0 236.2 jit_solution(13161146661799457511)
XLA Ops:
  0.7 0.7 convert_bitcast_fusion
  1.4 0.2 dynamic_update_slice.3.refs_4_
  1.6 0.0 copy-start
  1.6 0.6 copy-done
  2.2 100.3 %forward.1 = (bf16[8,96,2304]{2,1,0:T(8,128)(2,1)}, bf16[8,96,768]{2,1,0:T(8,128)(2,1)}, bf16[8,96,3072]{2,1,0:T(8,128)(2,1)}, bf16[8,384,768]{2,1,0:T(8,128)(2,...) custom-call(s32[2,1,4]{2,1,0:T(1,128)} %refs_0_.3, ...), custom_call_target="tpu_custom_call" | custom-call | tf_op jit(solution)/shard_map/forward/pallas_call | solution.py:876
  102.5 0.0 copy-start.2
  102.5 0.0 copy-start.4
  102.5 0.0 copy-start.3
  102.6 117.3 %backward.1 = (bf16[384,768]{1,0:T(8,128)(2,1)}, bf16[192,768]{1,0:T(8,128)(2,1)}, bf16[192,768]{1,0:T(8,128)(2,1)}, bf16[96,768]{1,0:T(8,128)(2,1)}, bf16[96,76...) custom-call(s32[2,1,4]{2,1,0:T(1,128)} %refs_0_.3, ...), custom_call_target="tpu_custom_call" | custom-call | tf_op jit(solution)/shard_map/backward/pallas_call | solution.py:1580
  219.9 0.0 copy-done.2
  219.9 0.0 copy-done.4
  219.9 1.4 fusion
  221.3 0.0 copy-start.1
  221.3 0.0 copy-done.3
  221.3 0.6 multiply_add_fusion
  221.9 14.1 %update.1 = (f32[96,6144]{1,0:T(8,128)}, f32[96,6144]{1,0:T(8,128)}, f32[96,6144]{1,0:T(8,128)}, f32[96,6144]{1,0:T(8,128)}, bf16[96,6144]{1,0:T(8,128)(2,1)}, /...) custom-call(bf16[384,768]{1,0:T(8,128)(2,1)} %get-tuple-element.83.r, ...), custom_call_target="tpu_custom_call" | custom-call | tf_op jit(solution)/shard_map/update/pallas_call | solution.py:1739
  236.0 0.0 copy-done.1
  (2 shorter events, 0.0 us)
Async XLA Ops:
  1.6 0.6 copy-start
  102.5 117.4 %copy-start.2 = (f32[96,12]{0,1:T(8,128)S(1)}, f32[96,12]{0,1:T(8,128)}, u32[]{:S(2)}) copy-start(f32[96,12]{0,1:T(8,128)} %param.23) | copy-start | bytes 13828
  102.5 117.4 %copy-start.4 = (f32[96,12]{0,1:T(8,128)S(1)}, f32[96,12]{0,1:T(8,128)}, u32[]{:S(2)}) copy-start(f32[96,12]{0,1:T(8,128)} %param.26) | copy-start | bytes 13828
  102.5 118.8 %copy-start.3 = (f32[96,12]{0,1:T(8,128)S(1)}, f32[96,12]{0,1:T(8,128)}, u32[]{:S(2)}) copy-start(f32[96,12]{0,1:T(8,128)} %param.29) | copy-start | bytes 13828
  221.3 14.7 %copy-start.1 = (f32[96,12]{0,1:T(8,128)}, f32[96,12]{0,1:T(8,128)S(1)}, u32[]{:S(2)}) copy-start(f32[96,12]{0,1:T(8,128)S(1)} %get-tuple-element.110) | copy-start | bytes 13828
where the time goes:
time: 237 us; the launch traced here: 236 us
  Pallas kernels  232 us (98%)
  other arithmetic  2.71 us (1%)
    pallas_call x1, Pallas kernels, backward(): pl.pallas_call(backward_kernel, in_specs=[smem, smem, vmem, vmem] + [any_...  117 us
    pallas_call x1, Pallas kernels, forward(): pl.pallas_call(forward_kernel, in_specs=[smem, smem, any_spec, any_spec,...  100 us
    pallas_call x1, Pallas kernels, update_all(): pl.pallas_call(update_kernel, grid=(UPDATE_STEPS,), in_specs=[vmem] * len...  14.1 us

commit v1 on v0

--- a/solution.py
+++ b/solution.py
@@ -592,24 +592,28 @@
     return j < jnp.where(j < 128, ends[0], jnp.where(j < 192, ends[1], ends[2]))
 
 
-DIRECT = (False, False, False, True)
-FIRST_JOBS = ((0, 1), (1, 0), (0, 2), (2, 0), (0, 3), (1, 1), (0, 4), (2, 1), (0, 5), (1, 2),)
+DIRECT = (True, False, False, False)
+FIRST_JOBS = ((4, 0), (0, 1), (1, 0), (0, 2), (2, 0), (0, 3), (0, 4), (1, 1),)
 PROJECT_JOBS = {
-    5: ((2, 2),),
-    7: ((1, 3),),
-    8: ((3, 0),),
+    0: ((2, 1),),
+    3: ((1, 2),),
+    4: ((2, 2),),
+    6: ((1, 3), (3, 0),),
 }
 ATTENTION_JOBS = {
     1: ((2, 3),),
-    2: ((1, 4),),
-    3: ((3, 1), (1, 5), (2, 4), (4, 0),),
-    5: ((2, 5),),
+    2: ((1, 4), (3, 1),),
+    3: ((2, 4),),
+    4: ((1, 5),),
+    5: ((3, 2), (2, 5),),
 }
-INNER_FIRST_JOBS = ((3, 2),)
+INNER_FIRST_JOBS = ()
 INNER_JOBS = {
-    2: ((3, 3),),
+    1: ((3, 3),),
+    2: ((3, 4),),
+    3: ((3, 5),),
 }
-OUTER_FIRST_JOBS = ((3, 4),)
+OUTER_FIRST_JOBS = ()
 
 
 def forward_kernel(*refs):
@@ -1225,7 +1229,7 @@
     (384, D, "xzy"),
     (192, D, "yxz"),
     (192, D, "xyz"),
-    (96, D, "xzy"),
+    (96, D, "zxy"),
     (96, D, "xzy"),
     (96, D, "xzy"),
     (96, D, "xzy"),
@@ -1233,27 +1237,27 @@
 
 
 MIDDLE_JOBS = {
-    0: (),
-    1: ((0, 30),),
-    2: ((0, 31),),
-    3: (),
+    0: ((0, 30),),
+    1: (),
+    2: ((0, 31), (1, 1), (1, 2),),
+    3: ((0, 32),),
 }
-ONE_JOBS = ((2, 1),)
-O_JOBS = ((1, 1),)
+ONE_JOBS = ((1, 30), (2, 1), (2, 2), (1, 31),)
+O_JOBS = ((0, 33), (2, 30), (3, 1), (1, 32), (3, 2),)
 BEFORE_PAIR = {
     0: (),
     1: (),
-    2: ((3, 1), (1, 2), (3, 2), (0, 32), (1, 30), (2, 2), (0, 33),),
-    3: ((1, 31), (4, 1),),
-    4: ((3, 31), (2, 30), (5, 1), (1, 33), (1, 40), (5, 2), (1, 41), (4, 30), (2, 31),),
-    5: ((2, 32), (2, 33), (5, 30), (2, 40), (5, 31), (0, 5),),
+    2: ((2, 32), (1, 33),),
+    3: ((4, 1),),
+    4: ((1, 41), (5, 1),),
+    5: ((4, 30), (4, 31), (0, 5), (5, 2),),
 }
 AFTER_GROUP = (
-    (),
-    ((4, 2), (0, 4), (3, 30), (1, 32),),
-    ((5, 32), (2, 41), (4, 31), (3, 32), (5, 33), (6, 1), (6, 2), (4, 32), (3, 33), (4, 33), (5, 4), (6, 30), (1, 42), (4, 4), (6, 31), (3, 4), (1, 43), (6, 32), (2, 42), (0, 6), (5, 5), (2, 43), (1, 5), (4, 5), (5, 6), (6, 33), (3, 5), (6, 4),),
+    ((0, 4), (2, 31),),
+    ((1, 40), (4, 2),),
+    ((5, 30), (5, 31), (2, 33),),
 )
-LAST_JOBS = ((1, 6), (2, 5), (3, 6), (6, 5), (2, 6), (4, 6), (6, 6),)
+LAST_JOBS = ((6, 1), (6, 2), (4, 32), (5, 32), (6, 30), (2, 40), (3, 3), (2, 41), (4, 33), (3, 4), (2, 42), (5, 33), (2, 43), (4, 4), (1, 42), (6, 31), (1, 43), (5, 4), (0, 6), (6, 32), (1, 5), (5, 5), (6, 33), (3, 5), (4, 5), (6, 4), (5, 6), (2, 5), (6, 5), (4, 6), (3, 6), (1, 6), (2, 6), (6, 6),)
 
 
 def backward_kernel(*refs):
@@ -1305,6 +1309,13 @@
     def act_chunk(k):
         return act_hbm.at[(z + k) % Z_CHIPS]
 
+    def up_chunk(k):
+        return jnp.where(k % 2 == 0, 1 - c, c) * 2 + k // 2
+
+    def slope_copy(k, slot):
+        rows = pl.ds(pl.multiple_of(up_chunk(k) * 256, 256), 256)
+        return pltpu.make_async_copy(slope_hbm.at[:, rows], big.at[slot].reshape(4, 256, D), big_sem.at[slot])
+
     chunk = lambda i: pl.ds(i * D, D)
     big_copy(act_chunk(1), 1).start()
     load_dfb = load(0, (dfb_hbm, dfb_s))
@@ -1353,7 +1364,7 @@
 
         @pl.when(k == Z_CHIPS)
         def _():
-            big_copy(slope_hbm.at[0], 1 - slot).start()
+            slope_copy(0, 1 - slot).start()
 
         for j, later in ((1, load_w2), (2, load_w1), (3, load_mid), (4, load_y1b + load_att)):
 
@@ -1386,34 +1397,68 @@
     def add(index, v):
         sums_s[index : index + 1, :] += jnp.sum(v, axis=0, keepdims=True)
 
-    def middle_back(r, carry):
-        slot = (r + 1) % 2
-        big_copy(slope_hbm.at[r], slot).wait()
-
-        @pl.when(r < 3)
+    done(load_y1b)
+    at_s[...] = jnp.transpose(y1b_s[...].reshape(1024, D))
+    load_tok = load(10, (tok_hbm, y1b_s))
+
+    def up_block(k, carry):
+        slot = (k + 1) % 2
+        slope_copy(k, slot).wait()
+
+        @pl.when(k < 3)
         def _():
-            big_copy(slope_hbm.at[r + 1], 1 - slot).start()
-
-        @pl.when(r == 0)
+            slope_copy(k + 1, 1 - slot).start()
+
+        @pl.when(k == 0)
         def _():
             down.z_block(Z_CHIPS)
-
-        during(r, MIDDLE_JOBS)
+            down.core_sent()
+
+        during(k, MIDDLE_JOBS)
+        chunk_rows = pl.ds(pl.multiple_of(up_chunk(k) * D, D), D)
+
+        def up_rows(r, carry):
+            slope = big[slot, pl.ds(pl.multiple_of(r * 256, 256), 256)].astype(f32)
+            dub = (dot_nt(dfb_s[r], second_s[chunk_rows]) * slope).astype(bf16)
+            dub_s[r] = dub
+            dh_s[r] += dot_nt(dub, first_s[chunk_rows])
+            return carry + jnp.sum(dub.astype(f32), axis=0, keepdims=True)
+
+        hidden_sum = lax.fori_loop(0, 4, up_rows, jnp.zeros((1, D), f32))
+        for j in range(4):
+
+            @pl.when(up_chunk(k) == j)
+            def _():
+                sums_s[8 + j : 9 + j, :] = hidden_sum
+
+        grad = dot_nn(at_s[...], dub_s[...].reshape(1024, D)).astype(bf16)
+        for e in range(2):
+            half = grad[:, e * (D // 2) : (e + 1) * (D // 2)].reshape(4, 2, 96, D // 2)
+            for j, ref in enumerate((one_a.theirs, one_a.acc, one_b.theirs, one_b.acc)):
+
+                @pl.when(k == j)
+                def _():
+                    ref[:, :, e * 96 : (e + 1) * 96, :] = half
+
+        for j, piece in ((0, one_a), (2, one_b)):
+
+            @pl.when(k == j)
+            def _():
+                piece.core_start()
+
+        return carry
+
+    lax.fori_loop(0, 4, up_block, 0)
+    run(ONE_JOBS)
+
+    def middle_back(r, carry):
         ainv_copy(r, r % 2).wait()
 
         @pl.when(r < 3)
         def _():
             ainv_copy(r + 1, (r + 1) % 2).start()
 
-        at = pl.ds(pl.multiple_of(r * 256, 256), 256)
-        dfb = dfb_s[r]
         dy1 = dh_s[r]
-        for k in range(FF // D):
-            slope = big[slot, k * 256 : (k + 1) * 256].astype(f32)
-            dub = (dot_nt(dfb, second_s[k * D : (k + 1) * D]) * slope).astype(bf16)
-            dub_s[k, at] = dub
-            add(8 + k, dub.astype(f32))
-            dy1 = dy1 + dot_nt(dub, first_s[k * D : (k + 1) * D])
         normed = dob_s[r].astype(f32)
         add(3, dy1 * normed)
         add(4, dy1)
@@ -1426,6 +1471,8 @@
         return carry
 
     lax.fori_loop(0, 4, middle_back, 0)
+    one_a.core_sent()
+    one_b.core_sent()
     qkv_loads = load(1, *[(qkv_hbm.at[:, :, chunk(j)], first_s.at[pl.ds(j * 1024, 1024)].reshape(4, 256, D)) for j in range(3)])
     w_loads = load(4, *[(w_hbm.at[:, chunk(j)], second_s.at[chunk(j)]) for j in range(3)])
 
@@ -1433,36 +1480,6 @@
         return big_copy(probs_hbm.at[i], slot)
 
     probs_copy(0, 0).start()
-
-    done(load_y1b)
-    at_s[...] = jnp.transpose(y1b_s[...].reshape(1024, D))
-    load_tok = load(10, (tok_hbm, y1b_s))
-    down.core_sent()
-
-    def one_block(k, carry):
-        core = jnp.where(k < 2, 1 - c, c)
-        grad = dot_nn(at_s[...], dub_s[core * 2 + k % 2]).astype(bf16)
-        for e in range(2):
-            half = grad[:, e * (D // 2) : (e + 1) * (D // 2)].reshape(4, 2, 96, D // 2)
-            rows = pl.ds(e * 96, 96)
-            for j, ref in enumerate((one_a.theirs, one_b.theirs, one_a.acc, one_b.acc)):
-
-                @pl.when(k == j)
-                def _():
-                    ref[:, :, rows, :] = half
-
-        for j, piece in ((0, one_a), (1, one_b)):
-
-            @pl.when(k == j)
-            def _():
-                piece.core_start()
-
-        return carry
-
-    lax.fori_loop(0, 4, one_block, 0)
-    run(ONE_JOBS)
-    one_a.core_sent()
-    one_b.core_sent()
 
     def small_grad(piece, right):
         piece.theirs[...] = dot_nn(at_s[...], right(1 - c)).astype(bf16).reshape(4, 2, 96, D // 2)
@@ -1512,36 +1529,29 @@
                 sum_v = sum_v + jnp.sum(grads[2].astype(f32), axis=0, keepdims=True)
                 for j in range(3):
                     dst = pl.ds(pl.multiple_of(j * 256 + (i % 2) * PAIR, PAIR), PAIR)
-                    dqkv_s[:, first : first + rows, dst] = grads[j].reshape(4, rows, PAIR)
+                    dqkv_s[g, :, first : first + rows, dst] = grads[j].reshape(4, rows, PAIR)
             sums_s[0:1, lanes] = sum_q
             sums_s[1:2, lanes] = sum_v
             return carry
 
         lax.fori_loop(2 * g, 2 * g + 2, pair, 0)
-        small_grad(pieces[4 + g], lambda core: dqkv_s[:, :, columns(core)].reshape(1024, D // 2))
+        small_grad(pieces[4 + g], lambda core, g=g: dqkv_s[g, :, :, columns(core)].reshape(1024, D // 2))
         if g == 2:
             sums.stage(0)
-
-        def rows_back(r, carry, g=g):
-            total = dh_s[r]
+        run(AFTER_GROUP[g])
+
+    def rows_back(r, carry):
+        total = dh_s[r]
+        for g in range(3):
             for j in range(3):
                 total = total + dot_nt(
-                    dqkv_s[r, :, j * 256 : (j + 1) * 256], second_s[j * D : (j + 1) * D, g * 256 : (g + 1) * 256]
+                    dqkv_s[g, r, :, j * 256 : (j + 1) * 256], second_s[j * D : (j + 1) * D, g * 256 : (g + 1) * 256]
                 )
-            if g < 2:
-                dh_s[r] = total
-            else:
-                y1b_s[r] = total.astype(bf16)
-            return carry
-
-        if g == 2:
-            lax.fori_loop(0, 4, rows_back, 0)
-            backs.start()
-            run(AFTER_GROUP[g])
-        else:
-            run(AFTER_GROUP[g])
-            lax.fori_loop(0, 4, rows_back, 0)
-
+        y1b_s[r] = total.astype(bf16)
+        return carry
+
+    lax.fori_loop(0, 4, rows_back, 0)
+    backs.start()
     sums.stage(1)
     run(LAST_JOBS)
     sums.stage(2)
@@ -1600,11 +1610,11 @@
             vm((FF, D)),
             vm((FF, D)),
             vm((D, D)),
-            vm((4, 1024, D)),
+            vm(tok),
             vm(tok, f32),
             vm(tok),
             vm((4, 256, 128), f32),
-            vm(tok),
+            vm((3, 4, 256, D)),
             vm((16, D), f32),
             vm((4, 16, D), f32),
             vm((16, D), f32),
@@ -1679,7 +1689,7 @@
     return (velocity, averaged, updated, updated.astype(jnp.bfloat16))
 
 
-UPDATE_STEPS = 8
+UPDATE_STEPS = 4
 
 
 def update_kernel(*refs):
@@ -1697,22 +1707,23 @@
     i = pl.program_id(0)
     for src, dst in zip(passed, passed_out):
         dst[...] = src[...]
-    half = D // 2
-    for b in range(UPDATE_STEPS):
-
-        @pl.when(i == b)
+    half, width = D // 2, grad_s.shape[1] // D
+    for b in range(UPDATE_STEPS * width):
+        first = b % width * D
+
+        @pl.when(i == b // width)
         def _():
             if b < 3:
                 for g, low in enumerate((low_0, low_1, low_2)):
-                    grad_s[:, g * 256 : (g + 1) * 256] = low[:, b * 256 : (b + 1) * 256]
+                    grad_s[:, first + g * 256 : first + (g + 1) * 256] = low[:, b * 256 : (b + 1) * 256]
             elif b == 3:
-                grad_s[...] = o_low[...]
+                grad_s[:, first : first + D] = o_low[...]
             else:
                 rows, core = grad_s.shape[0], (b - 4) // 2
                 low = (one_a, one_b)[b % 2]
                 for k in range(2):
                     part = low[k * rows : (k + 1) * rows, core * half : (core + 1) * half]
-                    grad_s[:, k * half : (k + 1) * half] = part
+                    grad_s[:, first + k * half : first + (k + 1) * half] = part
 
     def step(grad, state, outs):
         master, moment, average = state
@@ -1729,8 +1740,9 @@
     rows, cols = wide[0].shape
     down_rows = down[0].shape[0]
     vmem = pl.BlockSpec(memory_space=pltpu.VMEM)
-    short_spec = pl.BlockSpec((1, 1, 64, D), lambda i: (i // 4, i % 4, 0, 0))
-    long_spec = pl.BlockSpec((1, 1, 64, D), lambda i: (i // 4, i % 4 // 2, i % 2, 0))
+    halves = UPDATE_STEPS // 2
+    short_spec = pl.BlockSpec((1, 4 // halves, 64, D), lambda i: (i // halves, i % halves, 0, 0))
+    long_spec = pl.BlockSpec((1, 2 // halves, 128, D), lambda i: (i // halves, i % halves, 0, 0))
     passed_specs = [short_spec, long_spec, short_spec, long_spec]
     shape = jax.ShapeDtypeStruct
     wide_spec = pl.BlockSpec((rows, cols // UPDATE_STEPS), lambda i: (0, i))
@@ -1744,7 +1756,7 @@
         out_shape=[shape((rows, cols), t) for t in types]
         + [shape((down_rows, D), t) for t in types]
         + [shape(p.shape, p.dtype) for p in passed],
-        scratch_shapes=[pltpu.VMEM((rows, D), bf16)],
+        scratch_shapes=[pltpu.VMEM((rows, cols // UPDATE_STEPS), bf16)],
         compiler_params=params(),
         name="update",
     )(*lows, *wide, *down, *passed)

time: 237 us -> 231 us (0.975)
  Pallas kernels: 232 us -> 226 us
    pallas_call x1, Pallas kernels: 117 us -> 112 us  [backward(): pl.pallas_call(backward_kernel, in_specs=[smem, smem, vmem, vmem] + [any_...]
where the time goes in v1:
time: 231 us; the launch traced here: 230 us
  Pallas kernels  226 us (98%)
  other arithmetic  2.71 us (1%)
    pallas_call x1, Pallas kernels, backward(): pl.pallas_call(backward_kernel, in_specs=[smem, smem, vmem, vmem] + [any_...  112 us
    pallas_call x1, Pallas kernels, forward(): pl.pallas_call(forward_kernel, in_specs=[smem, smem, any_spec, any_spec,...  100 us
    pallas_call x1, Pallas kernels, update_all(): pl.pallas_call(update_kernel, grid=(UPDATE_STEPS,), in_specs=[vmem] * len...  13.1 us

profile of v1, /device:TPU:0, one launch (start us, length us, event | category | flops | bytes accessed | tf_op | source)
XLA Modules:
  0.0 230.4 jit_solution(4827485307903098558)
XLA Ops:
  0.7 0.7 convert_bitcast_fusion
  1.4 0.2 dynamic_update_slice.3.refs_4_
  1.6 0.0 copy-start
  1.6 0.6 copy-done
  2.2 100.5 %forward.1 = (bf16[8,96,2304]{2,1,0:T(8,128)(2,1)}, bf16[8,96,768]{2,1,0:T(8,128)(2,1)}, bf16[8,96,3072]{2,1,0:T(8,128)(2,1)}, bf16[8,384,768]{2,1,0:T(8,128)(2,...) custom-call(s32[2,1,4]{2,1,0:T(1,128)} %refs_0_.3, ...), custom_call_target="tpu_custom_call" | custom-call | tf_op jit(solution)/shard_map/forward/pallas_call | solution.py:880
  102.7 0.0 copy-start.2
  102.7 0.0 copy-start.4
  102.7 0.0 copy-start.3
  102.7 112.4 %backward.1 = (bf16[384,768]{1,0:T(8,128)(2,1)}, bf16[192,768]{1,0:T(8,128)(2,1)}, bf16[192,768]{1,0:T(8,128)(2,1)}, bf16[96,768]{1,0:T(8,128)(2,1)}, bf16[96,76...) custom-call(s32[2,1,4]{2,1,0:T(1,128)} %refs_0_.3, ...), custom_call_target="tpu_custom_call" | custom-call | tf_op jit(solution)/shard_map/backward/pallas_call | solution.py:1590
  215.1 0.0 copy-done.2
  215.1 0.0 copy-done.4
  215.1 1.4 fusion
  216.5 0.0 copy-start.1
  216.5 0.0 copy-done.3
  216.6 0.6 multiply_add_fusion
  217.2 13.1 %update.1 = (f32[96,6144]{1,0:T(8,128)}, f32[96,6144]{1,0:T(8,128)}, f32[96,6144]{1,0:T(8,128)}, f32[96,6144]{1,0:T(8,128)}, bf16[96,6144]{1,0:T(8,128)(2,1)}, /...) custom-call(bf16[384,768]{1,0:T(8,128)(2,1)} %get-tuple-element.83.r, ...), custom_call_target="tpu_custom_call" | custom-call | tf_op jit(solution)/shard_map/update/pallas_call | solution.py:1751
  230.2 0.0 copy-done.1
  (2 shorter events, 0.0 us)
Async XLA Ops:
  1.6 0.6 copy-start
  102.7 112.5 %copy-start.2 = (f32[96,12]{0,1:T(8,128)S(1)}, f32[96,12]{0,1:T(8,128)}, u32[]{:S(2)}) copy-start(f32[96,12]{0,1:T(8,128)} %param.23) | copy-start | bytes 13828
  102.7 112.4 %copy-start.4 = (f32[96,12]{0,1:T(8,128)S(1)}, f32[96,12]{0,1:T(8,128)}, u32[]{:S(2)}) copy-start(f32[96,12]{0,1:T(8,128)} %param.26) | copy-start | bytes 13828
  102.7 113.9 %copy-start.3 = (f32[96,12]{0,1:T(8,128)S(1)}, f32[96,12]{0,1:T(8,128)}, u32[]{:S(2)}) copy-start(f32[96,12]{0,1:T(8,128)} %param.29) | copy-start | bytes 13828
  216.5 13.7 %copy-start.1 = (f32[96,12]{0,1:T(8,128)}, f32[96,12]{0,1:T(8,128)S(1)}, u32[]{:S(2)}) copy-start(f32[96,12]{0,1:T(8,128)S(1)} %get-tuple-element.110) | copy-start | bytes 13828

commit v2 on v1

--- a/solution.py
+++ b/solution.py
@@ -1540,7 +1540,8 @@
             sums.stage(0)
         run(AFTER_GROUP[g])
 
-    def rows_back(r, carry):
+    def rows_back(i, carry):
+        r = (s + 1 + i) % 4
         total = dh_s[r]
         for g in range(3):
             for j in range(3):
@@ -1548,10 +1549,18 @@
                     dqkv_s[g, r, :, j * 256 : (j + 1) * 256], second_s[j * D : (j + 1) * D, g * 256 : (g + 1) * 256]
                 )
         y1b_s[r] = total.astype(bf16)
+        for k in range(1, 4):
+
+            @pl.when(i == k - 1)
+            def _():
+                for copy in backs.copies(k):
+                    copy.start()
+
         return carry
 
     lax.fori_loop(0, 4, rows_back, 0)
-    backs.start()
+    for copy in backs.own():
+        copy.start()
     sums.stage(1)
     run(LAST_JOBS)
     sums.stage(2)

time: 231 us -> 230 us (level)
  no operation moved by 1% of the time
where the time goes in v2:
time: 230 us
  Pallas kernels  225 us (98%)
  other arithmetic  2.71 us (1%)
    pallas_call x1, Pallas kernels, backward(): pl.pallas_call(backward_kernel, in_specs=[smem, smem, vmem, vmem] + [any_...  112 us
    pallas_call x1, Pallas kernels, forward(): pl.pallas_call(forward_kernel, in_specs=[smem, smem, any_spec, any_spec,...  100 us
    pallas_call x1, Pallas kernels, update_all(): pl.pallas_call(update_kernel, grid=(UPDATE_STEPS,), in_specs=[vmem] * len...  13.1 us

profile of v2, /device:TPU:0, one launch (start us, length us, event | category | flops | bytes accessed | tf_op | source)
XLA Modules:
  0.0 229.8 jit_solution(158427514156530733)
XLA Ops:
  0.7 0.7 convert_bitcast_fusion
  1.4 0.2 dynamic_update_slice.3.refs_4_
  1.6 0.0 copy-start
  1.6 0.6 copy-done
  2.2 100.5 %forward.1 = (bf16[8,96,2304]{2,1,0:T(8,128)(2,1)}, bf16[8,96,768]{2,1,0:T(8,128)(2,1)}, bf16[8,96,3072]{2,1,0:T(8,128)(2,1)}, bf16[8,384,768]{2,1,0:T(8,128)(2,...) custom-call(s32[2,1,4]{2,1,0:T(1,128)} %refs_0_.3, ...), custom_call_target="tpu_custom_call" | custom-call | tf_op jit(solution)/shard_map/forward/pallas_call | solution.py:880
  102.7 0.0 copy-start.2
  102.7 0.0 copy-start.4
  102.7 0.0 copy-start.3
  102.7 111.8 %backward.1 = (bf16[384,768]{1,0:T(8,128)(2,1)}, bf16[192,768]{1,0:T(8,128)(2,1)}, bf16[192,768]{1,0:T(8,128)(2,1)}, bf16[96,768]{1,0:T(8,128)(2,1)}, bf16[96,76...) custom-call(s32[2,1,4]{2,1,0:T(1,128)} %refs_0_.3, ...), custom_call_target="tpu_custom_call" | custom-call | tf_op jit(solution)/shard_map/backward/pallas_call | solution.py:1599
  214.5 0.0 copy-done.2
  214.5 0.0 copy-done.4
  214.5 1.4 fusion
  215.9 0.0 copy-start.1
  215.9 0.0 copy-done.3
  215.9 0.6 multiply_add_fusion
  216.5 13.1 %update.1 = (f32[96,6144]{1,0:T(8,128)}, f32[96,6144]{1,0:T(8,128)}, f32[96,6144]{1,0:T(8,128)}, f32[96,6144]{1,0:T(8,128)}, bf16[96,6144]{1,0:T(8,128)(2,1)}, /...) custom-call(bf16[384,768]{1,0:T(8,128)(2,1)} %get-tuple-element.83.r, ...), custom_call_target="tpu_custom_call" | custom-call | tf_op jit(solution)/shard_map/update/pallas_call | solution.py:1760
  229.6 0.0 copy-done.1
  (2 shorter events, 0.0 us)
Async XLA Ops:
  1.6 0.6 copy-start
  102.7 111.8 %copy-start.2 = (f32[96,12]{0,1:T(8,128)S(1)}, f32[96,12]{0,1:T(8,128)}, u32[]{:S(2)}) copy-start(f32[96,12]{0,1:T(8,128)} %param.23) | copy-start | bytes 13828
  102.7 111.8 %copy-start.4 = (f32[96,12]{0,1:T(8,128)S(1)}, f32[96,12]{0,1:T(8,128)}, u32[]{:S(2)}) copy-start(f32[96,12]{0,1:T(8,128)} %param.26) | copy-start | bytes 13828
  102.7 113.2 %copy-start.3 = (f32[96,12]{0,1:T(8,128)S(1)}, f32[96,12]{0,1:T(8,128)}, u32[]{:S(2)}) copy-start(f32[96,12]{0,1:T(8,128)} %param.29) | copy-start | bytes 13828
  215.9 13.7 %copy-start.1 = (f32[96,12]{0,1:T(8,128)}, f32[96,12]{0,1:T(8,128)S(1)}, u32[]{:S(2)}) copy-start(f32[96,12]{0,1:T(8,128)S(1)} %get-tuple-element.110) | copy-start | bytes 13828
